TPU v7x, 256 devices: a whole 4x4x8 slice. The times are simulated.
256 devices in a mesh: grp: 16 (over z_lo, x), tp: 16 (over z_hi, y, core).
Axes of the slice: x: 4, y: 4, z: 8 (z_hi: 2, z_lo: 4; z = z_hi * 4 + z_lo), core: 2. Of those that a mesh axis runs over, the one named last changes fastest.
Arguments:
- inputs: bfloat16 [4, 512, 8192], P(None, 'grp'), may hold values from -6 to 6
- norm_gain: bfloat16 [8192], replicated, may hold values from 0.5 to 1.5
- w_query: bfloat16 [8192, 8, 512], P(None, None, 'tp')
- w_keyval: bfloat16 [8192, 2, 512], P(None, None, 'tp')
- w_out: bfloat16 [8, 512, 8192], P(None, 'tp'), may hold values from -1.5 to 1.5
- kv_cache: bfloat16 [2, 512, 512, 512], P(None, 'grp', 'tp'), may hold values from -127 to 127, as said below
- kv_scales: bfloat16 [2, 512, 16, 512], P(None, 'grp', 'tp'), may hold values from 0.004 to 1.2
- ancestors: int32 [512], replicated, may hold values from 0 to 511, as said below
Outputs:
- attn_out: bfloat16 [4, 512, 8192], P(None, 'grp', 'tp')
Inputs may be any that keep to these rules, and one draw needn't show every extreme that they name: Particle p takes over the cache of particle ancestors[p]. Among the 32 particles of one group, at most 4 have ancestors in any one group (their own included), and exactly 4 in some group. `kv_cache`: whole numbers.
All inputs are finite; a program needn't handle non-finite values.
Results may differ from a plain program's by a relative error of at most 0.015.
The roundings to bfloat16 on the way count: a program that leaves them out, or rounds other values in their place, can miss the bound.
Values may be sent and summed in bfloat16 or wider, within the bound.
A program may use at most 128 MiB of HBM per device.

v0:
```python
import jax
import jax.numpy as jnp
from jax import lax
from jax.sharding import PartitionSpec as P

HD = 128
KVH = 4
CAP = 4


def partner_2(value, axis, distance):
    mask = 2**distance
    pairs = [(source, source ^ mask) for source in range(lax.axis_size(axis))]
    return lax.ppermute(value, axis, pairs)


def rotate_pairs(values, offset, step_count, cached):
    length = values.shape[-1]
    blocks = length // 32
    block_ids = offset // 32 + jnp.arange(blocks)
    within = jnp.arange(16)
    pair_index = (block_ids % (HD // 32))[:, None] * 16 + within[None, :]
    frequency = jnp.exp(
        -(pair_index.astype(jnp.float32) / (HD // 2)) * jnp.log(jnp.float32(500000.0))
    )
    positions = (cached + jnp.arange(step_count)).astype(jnp.float32)
    angles = positions[:, None, None] * frequency[None]
    ones_shape = (1,) * (values.ndim - 2)
    cosine = jnp.cos(angles).reshape((step_count,) + ones_shape + (blocks, 16))
    sine_part = jnp.sin(angles).reshape((step_count,) + ones_shape + (blocks, 16))
    shaped = values.reshape(values.shape[:-1] + (blocks, 2, 16))
    front_half = shaped[..., 0, :]
    back_half = shaped[..., 1, :]
    new_front = front_half * cosine - back_half * sine_part
    new_back = back_half * cosine + front_half * sine_part
    return jnp.stack([new_front, new_back], -2).reshape(values.shape)


def softmax_parts(cache_scores, new_scores):
    step_count = new_scores.shape[0]
    visible = jnp.arange(step_count)[None, :] <= jnp.arange(step_count)[:, None]
    visible = visible.reshape((step_count,) + (1,) * (new_scores.ndim - 2) + (step_count,))
    masked = jnp.where(visible, new_scores, -jnp.inf)
    highest = jnp.maximum(
        jnp.max(cache_scores, -1, keepdims=True), jnp.max(masked, -1, keepdims=True)
    )
    cache_exp = jnp.exp(cache_scores - highest)
    new_exp = jnp.exp(masked - highest)
    total = jnp.sum(cache_exp, -1, keepdims=True) + jnp.sum(new_exp, -1, keepdims=True)
    return ((cache_exp / total).astype(jnp.bfloat16), (new_exp / total).astype(jnp.bfloat16))


def attend(query, new_key, new_value, caches, scales, bit_count):
    step_count, row_count, heads, feature_count = query.shape
    cached = caches.shape[3]
    block_count = feature_count // 32
    key_ints = caches[0].reshape(row_count, block_count, 32, cached)
    key_scale = scales[0].astype(jnp.float32)
    q_blocks = query.reshape(step_count, row_count, heads, block_count, 32)
    partial_value = jnp.einsum(
        "spgnf,pnfl->spgnl", q_blocks, key_ints, preferred_element_type=jnp.float32
    )
    cache_scores = jnp.sum(partial_value * key_scale[None, :, None], axis=3)
    new_scores = jnp.einsum("spgf,tpf->spgt", query, new_key, preferred_element_type=jnp.float32)
    for bit_number in range(bit_count):
        partner = partner_2((cache_scores, new_scores), "tp", bit_number)
        cache_scores = cache_scores + partner[0]
        new_scores = new_scores + partner[1]
    cache_probs, new_probs = softmax_parts(cache_scores, new_scores)
    value_ints = caches[1].reshape(row_count, block_count, 32, cached)
    value_scale = scales[1].astype(jnp.float32)
    weighted = (
        cache_probs.astype(jnp.float32)[:, :, :, None, :] * value_scale[None, :, None]
    ).astype(jnp.bfloat16)
    from_cache = jnp.einsum(
        "spgnl,pnfl->spgnf", weighted, value_ints, preferred_element_type=jnp.float32
    )
    from_new = jnp.einsum(
        "spgt,tpf->spgf", new_probs, new_value, preferred_element_type=jnp.float32
    )
    return (from_cache.reshape(step_count, row_count, heads, feature_count) + from_new).astype(
        jnp.bfloat16
    )


def shards(inputs, norm_gain, w_query, w_keyval, w_out, kv_cache, kv_scales, ancestors):
    step_count, particles, width = inputs.shape
    feature_count = w_query.shape[2]
    cached = kv_cache.shape[3]
    tp_rank = lax.axis_index("tp")
    offset = tp_rank * feature_count
    bit_count = (lax.axis_size("tp") // KVH).bit_length() - 1
    floats = inputs.astype(jnp.float32)
    normed = (
        floats
        * lax.rsqrt(jnp.mean(floats * floats, axis=-1, keepdims=True) + 1e-05)
        * norm_gain.astype(jnp.float32)
    ).astype(jnp.bfloat16)
    query = jnp.einsum("spd,dgf->spgf", normed, w_query, preferred_element_type=jnp.float32)
    query = (rotate_pairs(query, offset, step_count, cached) * HD ** (-0.5)).astype(jnp.bfloat16)
    keyval = jnp.einsum("spd,dcf->spcf", normed, w_keyval, preferred_element_type=jnp.float32)
    new_key = rotate_pairs(keyval[:, :, 0], offset, step_count, cached).astype(jnp.bfloat16)
    new_value = keyval[:, :, 1].astype(jnp.bfloat16)
    group_count = lax.axis_size("grp")
    my_group = lax.axis_index("grp")
    parents = ancestors.reshape(group_count, particles)
    source = parents // particles
    parent_slot = parents % particles
    child_ids = jnp.arange(particles)
    earlier = child_ids[None, :] < child_ids[:, None]
    sibling_rank = jnp.sum((source[:, :, None] == source[:, None, :]) & earlier[None], axis=2)
    slot_ids = jnp.arange(CAP)
    matches = (source[:, None, :] == my_group) & (
        sibling_rank[:, None, :] == slot_ids[None, :, None]
    )
    picked = jnp.sum(jnp.where(matches, parent_slot[:, None, :], 0), axis=2).reshape(-1)
    my_source = lax.dynamic_index_in_dim(source, my_group, 0, keepdims=False)
    my_rank = lax.dynamic_index_in_dim(sibling_rank, my_group, 0, keepdims=False)
    lookup = my_source * CAP + my_rank
    host_rows = group_count * CAP
    outgoing = (
        jnp.take(kv_cache, picked, axis=1).reshape((2, group_count, CAP) + kv_cache.shape[2:]),
        jnp.take(kv_scales, picked, axis=1).reshape((2, group_count, CAP) + kv_scales.shape[2:]),
    )
    arrived = (
        lax.all_to_all(outgoing[0], "grp", split_axis=1, concat_axis=1, tiled=True),
        lax.all_to_all(outgoing[1], "grp", split_axis=1, concat_axis=1, tiled=True),
    )
    caches = jnp.take(arrived[0].reshape((2, host_rows) + kv_cache.shape[2:]), lookup, axis=1)
    scales = jnp.take(arrived[1].reshape((2, host_rows) + kv_scales.shape[2:]), lookup, axis=1)
    mixed = attend(query, new_key, new_value, caches, scales, bit_count)
    term = jnp.einsum("spgf,gfd->spd", mixed, w_out, preferred_element_type=jnp.float32)
    return lax.psum_scatter(term, "tp", scatter_dimension=2, tiled=True).astype(jnp.bfloat16)


def solution(mesh):
    in_specs = (
        P(None, "grp", None),
        P(),
        P(None, None, "tp"),
        P(None, None, "tp"),
        P(None, "tp", None),
        P(None, "grp", "tp", None),
        P(None, "grp", "tp", None),
        P(),
    )
    out_specs = P(None, "grp", "tp")
    return jax.shard_map(shards, mesh=mesh, in_specs=in_specs, out_specs=out_specs, check_vma=False)
```

profile of v0, /device:TPU:2, one launch (start us, length us, event | category | flops | bytes accessed | tf_op | source)
XLA Modules:
  0.0 322.0 jit_solution(4697556336153621393)
XLA Ops:
  6.5 0.9 reshape.449
  8.4 0.9 copy.98
  9.3 0.8 gather_fusion.2
  10.2 0.9 broadcast_select_fusion.1
  11.0 8.9 %all-to-all-start.1 = ((bf16[2,16,4,1,512]{4,0,2,3,1:T(2,128)(2,1)}), bf16[2,16,4,1,512]{4,0,2,3,1:T(2,128)(2,1)S(1)}, u32[]{:S(2)}, u32[]{:S(2)}) async-start(bf16[2,16,4,1,512]{4,0,2,3,1:T(2,128)(2,1)} %broadcast_select_fusion.1), calls=%async_computation.1 | async-start | bytes 262144 | tf_op jit(solution)/shard_map/all_to_all | solution.py:127
  19.9 2.8 gather_fusion
  22.7 2.5 copy.59
  25.2 0.5 broadcast_select_fusion
  25.7 2.3 copy.60
  27.9 7.7 %all-to-all-start = ((bf16[2,16,4,32,512]{4,3,2,0,1:T(8,128)(2,1)}), bf16[2,16,4,32,512]{4,3,2,0,1:T(8,128)(2,1)}, u32[]{:S(2)}, u32[]{:S(2)}) async-start(bf16[2,16,4,32,512]{4,3,2,0,1:T(8,128)(2,1)} %copy.60), calls=%async_computation | async-start | bytes 8388608 | tf_op jit(solution)/shard_map/all_to_all | solution.py:126
  35.7 2.2 fusion
  38.1 5.3 %fusion.4 = f32[4,32,8,32]{1,3,2,0:T(8,128)S(1)} fusion(bf16[8192,8,32]{0,2,1:T(8,128)(2,1)} %param.10, bf16[4,32,8192]{2,1,0:T(8,128)(2,1)S(1)} %copy-done.3, f32[8192]{0:T(1024)S(1)} %convert_element_type.91, f32[4,32]{1,0:T(4,128)S(1)} %add_rsqrt_fusion), kind=kOutput, calls=%fused_computation.11 | convolution fusion | flops 541065216 | bytes 6455808 | tf_op jit(solution)/shard_map/spd,dgf->spgf/dot_general | solution.py:99
  44.1 0.7 gather_fusion.3
  45.0 68.5 %all-to-all-done = bf16[2,16,4,32,512]{4,3,2,0,1:T(8,128)(2,1)} async-done(((bf16[2,16,4,32,512]{4,3,2,0,1:T(8,128)(2,1)}), bf16[2,16,4,32,512]{4,3,2,0,1:T(8,128)(2,1)}, u32[]{:S(2)}, u32[]{:S(2)}) %all-to-all-start) | async-done | bytes 4194336 | tf_op jit(solution)/shard_map/all_to_all | solution.py:126
  113.6 4.7 %copy.61 = bf16[2,16,4,32,512]{4,3,2,1,0:T(8,128)(2,1)} copy(bf16[2,16,4,32,512]{4,3,2,0,1:T(8,128)(2,1)} %all-to-all-done) | data formatting | bytes 8388608 | tf_op jit(solution)/shard_map/all_to_all | solution.py:126
  118.3 4.2 %gather_fusion.1 = bf16[32,2,32,512]{3,2,1,0:T(8,128)(2,1)} fusion(bf16[2,64,32,512]{3,2,1,0:T(8,128)(2,1)} %bitcast.101, s32[1024]{0:T(1024)S(1)} %pad_clamp_fusion), kind=kCustom, calls=%fused_computation.1 | custom fusion | bytes 4194432 | tf_op jit(solution)/shard_map/jit(_take)/gather | solution.py:129
  122.5 1.8 fusion.8
  124.9 4.1 %collective-permute-done = f32[4,32,8,512]{3,2,0,1:T(8,128)S(1)} collective-permute-done((f32[4,32,8,512]{3,2,0,1:T(8,128)S(1)}, f32[4,32,8,512]{3,2,0,1:T(8,128)S(1)}, u32[]{:S(2)}, u32[]{:S(2)}) %collective-permute-start) | collective-permute-done | bytes 2097184 | tf_op jit(solution)/shard_map/ppermute | solution.py:14
  129.1 1.8 add.207
  130.8 1.6 collective-permute-start.1
  132.4 1.0 fusion.12
  133.8 1.2 convolution_bitcast_fusion.3
  135.0 1.5 collective-permute-done.2
  136.6 0.7 collective-permute-start.3
  137.4 47.0 %collective-permute-done.3 = f32[4,32,8,4]{2,3,0,1:T(4,128)S(1)} collective-permute-done((f32[4,32,8,4]{2,3,0,1:T(4,128)S(1)}, f32[4,32,8,4]{2,3,0,1:T(4,128)S(1)}, u32[]{:S(2)}, u32[]{:S(2)}) %collective-permute-start.3) | collective-permute-done | bytes 16416 | tf_op jit(solution)/shard_map/ppermute | solution.py:14
  184.7 2.5 fusion.30
  187.5 0.8 fusion.9
  189.1 0.6 fusion.11
  189.7 1.5 copy-done.6
  191.3 3.3 %convolution_bitcast_fusion = f32[4,32,8192]{2,1,0:T(8,128)} fusion(bf16[8,32,8192]{2,1,0:T(8,128)(2,1)S(1)} %copy-done.6, bf16[4,32,8,32]{3,2,0,1:T(8,128)(2,1)S(1)} %fusion.11), kind=kOutput, calls=%fused_computation.4 | convolution fusion | flops 536870912 | bytes 8454144 | tf_op jit(solution)/shard_map/spgf,gfd->spd/dot_general | solution.py:132
  194.6 118.9 %reduce-scatter.2.cloned.1.call-done = f32[4,32,512]{2,1,0:T(8,128)} async-done(((f32[4,32,8192]{2,1,0:T(8,128)}), f32[4,32,512]{2,1,0:T(8,128)}) %reduce-scatter.2.cloned.1.call-update) | async-done | bytes 262160 | tf_op jit(solution)/shard_map/reduce_scatter | solution.py:133
  313.5 1.6 convert_element_type.108
  (61 shorter events, 4.3 us)
Async XLA Ops:
  6.5 13.4 %copy-start = (bf16[2,32,32,512]{3,2,1,0:T(8,128)(2,1)S(1)}, bf16[2,32,32,512]{3,2,1,0:T(8,128)(2,1)}, u32[]{:S(2)}) copy-start(bf16[2,32,32,512]{3,2,1,0:T(8,128)(2,1)} %param.13) | copy-start | bytes 6291460
  11.0 16.9 %all-to-all-start.1 = ((bf16[2,16,4,1,512]{4,0,2,3,1:T(2,128)(2,1)}), bf16[2,16,4,1,512]{4,0,2,3,1:T(2,128)(2,1)S(1)}, u32[]{:S(2)}, u32[]{:S(2)}) async-start(bf16[2,16,4,1,512]{4,0,2,3,1:T(2,128)(2,1)} %broadcast_select_fusion.1), calls=%async_computation.1 | async-start | bytes 262144 | tf_op jit(solution)/shard_map/all_to_all | solution.py:127
  27.9 7.7 %copy-start.5 = (bf16[8192]{0:T(1024)(128)(2,1)S(1)}, bf16[8192]{0:T(1024)(128)(2,1)}, u32[]{:S(2)}) copy-start(bf16[8192]{0:T(1024)(128)(2,1)} %param.9) | copy-start | bytes 49156
  27.9 85.6 %all-to-all-start = ((bf16[2,16,4,32,512]{4,3,2,0,1:T(8,128)(2,1)}), bf16[2,16,4,32,512]{4,3,2,0,1:T(8,128)(2,1)}, u32[]{:S(2)}, u32[]{:S(2)}) async-start(bf16[2,16,4,32,512]{4,3,2,0,1:T(8,128)(2,1)} %copy.60), calls=%async_computation | async-start | bytes 8388608 | tf_op jit(solution)/shard_map/all_to_all | solution.py:126
  35.6 277.9 %reduce-scatter.2.cloned.1.call-start = ((), (), s32[]{:S(2)}) async-start(), calls=%async_computation.3 | async-start | bytes 4456448 | tf_op jit(solution)/shard_map/reduce_scatter | solution.py:133
  35.7 2.4 copy-start.3
  124.3 6.5 %copy-start.1 = (bf16[2,32,32,512]{3,2,1,0:T(8,128)(2,1)}, bf16[2,32,32,512]{3,2,1,0:T(8,128)(2,1)S(1)}, u32[]{:S(2)}) copy-start(bf16[2,32,32,512]{3,2,1,0:T(8,128)(2,1)S(1)} %fusion.8) | copy-start | bytes 6291460
  124.8 7.6 %copy-start.4 = (bf16[4,32,8192]{2,1,0:T(8,128)(2,1)S(1)}, bf16[4,32,8192]{2,1,0:T(8,128)(2,1)}, u32[]{:S(2)}) copy-start(bf16[4,32,8192]{2,1,0:T(8,128)(2,1)} %param.8) | copy-start | bytes 6291460
  124.8 7.6 %copy-start.7 = (bf16[8192,2,32]{0,2,1:T(8,128)(2,1)S(1)}, bf16[8192,2,32]{0,2,1:T(8,128)(2,1)}, u32[]{:S(2)}) copy-start(bf16[8192,2,32]{0,2,1:T(8,128)(2,1)} %param.11) | copy-start | bytes 3145732
  124.8 4.2 %collective-permute-start = (f32[4,32,8,512]{3,2,0,1:T(8,128)S(1)}, f32[4,32,8,512]{3,2,0,1:T(8,128)S(1)}, u32[]{:S(2)}, u32[]{:S(2)}) collective-permute-start(f32[4,32,8,512]{3,2,0,1:T(8,128)S(1)} %fusion.7), channel_id=1, source_target_pairs={{0,1},{1,0},{2,3},{3,2},{4,5},{5,4},{6,7},{7,6},{8,9},{9,8},{10,11... | collective-permute-start | bytes 6291464 | tf_op jit(solution)/shard_map/ppermute | solution.py:14
  130.8 53.8 %collective-permute-start.1 = (f32[4,32,8,512]{3,2,0,1:T(8,128)}, f32[4,32,8,512]{3,2,0,1:T(8,128)}, u32[]{:S(2)}, u32[]{:S(2)}) collective-permute-start(f32[4,32,8,512]{3,2,0,1:T(8,128)} %add.207), channel_id=1, source_target_pairs={{0,2},{1,3},{2,0},{3,1},{4,6},{5,7},{6,4},{7,5},{8,10},{9,11},{10,... | collective-permute-start | bytes 6291464 | tf_op jit(solution)/shard_map/ppermute | solution.py:14
  135.0 1.6 collective-permute-start.2
  136.6 47.7 %collective-permute-start.3 = (f32[4,32,8,4]{2,3,0,1:T(4,128)S(1)}, f32[4,32,8,4]{2,3,0,1:T(4,128)S(1)}, u32[]{:S(2)}, u32[]{:S(2)}) collective-permute-start(f32[4,32,8,4]{2,3,0,1:T(4,128)S(1)} %add.210), channel_id=1, source_target_pairs={{0,2},{1,3},{2,0},{3,1},{4,6},{5,7},{6,4},{7,5},{8,10},{9,11},{10,... | collective-permute-start | bytes 49160 | tf_op jit(solution)/shard_map/ppermute | solution.py:14
  187.5 1.6 copy-start.2
  189.1 2.2 copy-start.6
Sparse Core Ops, SparseCore 0:
  194.7 118.7 reduce-scatter.1
where the time goes:
time: 323 us; the launch traced here: 322 us
  waiting for transfers between devices  240 us (74%)
  local copies, waits for them, and re-layouts  22.7 us (7%)
  starting transfers between devices  19 us (6%)
  other arithmetic  14.2 us (4%)
  between operations  13.8 us (4%)
  matrix products  12.2 us (4%)
    reduce_scatter x1, waiting for transfers between devices, shards(): lax.psum_scatter(term, 'tp', scatter_dimension=2, tiled=True)  119 us
    all_to_all x1, waiting for transfers between devices, shards(): lax.all_to_all(outgoing[0], 'grp', split_axis=1, concat_axis=1, tiled=True)  68.5 us
    ppermute x4, waiting for transfers between devices, partner_2(): return lax.ppermute(value, axis, pairs)  52.6 us
    all_to_all x1, starting transfers between devices, shards(): lax.all_to_all(outgoing[1], 'grp', split_axis=1, concat_axis=1, tiled=True)  8.91 us
    all_to_all x1, starting transfers between devices, shards(): lax.all_to_all(outgoing[0], 'grp', split_axis=1, concat_axis=1, tiled=True)  7.65 us
  transfers between devices with their start and end apart: 7, of which 5 were waited for; matrix products, arithmetic and copies ran while one was open for 6% of the time, Pallas kernels for 0%

commit v1 on v0

v1 whole, which is shorter than its diff:
```python
import functools

import jax
import jax.numpy as jnp
import numpy as np
from jax import lax
from jax.experimental import pallas as pl
from jax.experimental.pallas import tpu as pltpu
from jax.sharding import PartitionSpec as P

HD = 128
CAP = 4
MESH = pl.DeviceIdType.MESH
F32 = jnp.float32
BF16 = jnp.bfloat16
MAX_CHUNKS = 4
BLOCKS = ((0, 2), (1, 2), (0, 1), (1, 3), (0, 3), (1, 1), (0, 0), (1, 0))


def flip(t, bit):
    return t + bit - 2 * bit * ((t // bit) % 2)


def mate(t, offset):
    if offset & 1:
        t = flip(t, 1)
    if offset & 2:
        t = flip(t, 2)
    return t


def nt(a, b):
    return lax.dot_general(a, b, (((1,), (1,)), ((), ())), preferred_element_type=F32)


def nn(a, b):
    return jnp.dot(a, b, preferred_element_type=F32)


def iota(shape, axis):
    return lax.broadcasted_iota(jnp.int32, shape, axis)


def kernel(
    ng, x_hbm, gain_ref, wq_hbm, wkv_hbm, wo_hbm, kv_hbm, sc_hbm, rope_ref, child_ref, col_ref, ids_ref,
    out_ref,
    xv, wv, wov, accq, qt, onehot, spread, sendq, qx, kx, vx, scx, scf, prob, pnew, stat, st_send, st_recv,
    fac, acc, ra, sb, rb, mix, back, fold, ta_send, ta_recv, own, tb_send, tb_recv, fin, tc_send, tc_recv,
    loc_sem, kv_ssem, kv_rsem, qa_ssem, qa_rsem, qg_ssem, qg_rsem, st_ssem, st_rsem, ha_ssem, ha_rsem,
    hb_ssem, hb_rsem, bk_ssem, bk_rsem, ta_ssem, ta_rsem, tb_ssem, tb_rsem, tc_ssem, tc_rsem,
):
    g = lax.axis_index("grp")
    t = lax.axis_index("tp")
    i = t % 4
    core = t % 2
    yb = (t // 2) % 2
    y = (t // 2) % 4
    zh = t // 8
    width = x_hbm.shape[1]
    cb = out_ref.shape[1]
    chunks = min(MAX_CHUNKS, ng)
    per = ng // chunks

    loads = [
        pltpu.make_async_copy(x_hbm, xv, loc_sem.at[0]),
        pltpu.make_async_copy(wq_hbm, wv.at[pl.ds(0, 256)], loc_sem.at[1]),
        pltpu.make_async_copy(wkv_hbm, wv.at[pl.ds(256, 64)], loc_sem.at[2]),
        pltpu.make_async_copy(wo_hbm, wov, loc_sem.at[3]),
    ]
    for copy in loads[:3]:
        copy.start()

    barrier = pltpu.get_barrier_semaphore()
    tp_peers = [mate(t, 1), mate(t, 2), mate(t, 3), t + 2 * ((y + 3 - 2 * (y % 2)) % 4 - y), flip(t, 8)]

    def greet(k, _):
        pl.semaphore_signal(barrier, inc=1, device_id={"grp": lax.rem(g + k, ng)}, device_id_type=MESH)
        return 0

    for peer in tp_peers:
        pl.semaphore_signal(barrier, inc=1, device_id={"tp": peer}, device_id_type=MESH)
    lax.fori_loop(1, ng, greet, 0)
    pl.semaphore_wait(barrier, len(tp_peers) + ng - 1)

    def cache_copies(offset):
        other = mate(t, offset)
        lanes = pl.ds(pl.multiple_of(128 * (other % 4), 128), 128)
        o = offset - 1
        args = dict(device_id={"tp": other}, device_id_type=MESH)
        return [
            pltpu.make_async_remote_copy(
                kv_hbm.at[0, :, :, lanes], kx.at[i], kv_ssem.at[o, 0], kv_rsem.at[o, 0], **args),
            pltpu.make_async_remote_copy(
                sc_hbm.at[:, :, lanes], scx.at[i], kv_ssem.at[o, 1], kv_rsem.at[o, 1], **args),
            pltpu.make_async_remote_copy(
                kv_hbm.at[1, :, :, lanes], vx.at[i], kv_ssem.at[o, 2], kv_rsem.at[o, 2], **args),
        ]

    cache_moves = [cache_copies(o) for o in (1, 2, 3)]
    for kind in range(3):
        for o in (2, 1, 0):
            cache_moves[o][kind].start()
    mine = pl.ds(pl.multiple_of(128 * i, 128), 128)
    own_cache = [
        pltpu.make_async_copy(kv_hbm.at[0, :, :, mine], kx.at[i], loc_sem.at[4]),
        pltpu.make_async_copy(sc_hbm.at[:, :, mine], scx.at[i], loc_sem.at[5]),
        pltpu.make_async_copy(kv_hbm.at[1, :, :, mine], vx.at[i], loc_sem.at[6]),
    ]
    for copy in own_cache:
        copy.start()
    loads[3].start()

    rows = ng * 16
    row = iota((rows, 128), 0)
    lane = iota((rows, 128), 1)
    for c in range(CAP):
        hit = (child_ref[:, c : c + 1] == lane % 32) & (row % 4 == lane // 32)
        for gl in range(4):
            block = jnp.where(hit & ((row // 4) % 4 == gl), 1.0, 0.0).astype(BF16)
            onehot[:, (c * 4 + gl) * 128 : (c * 4 + gl + 1) * 128] = block
    spread[...] = jnp.zeros_like(spread)

    loads[0].wait()
    step = min(1024, width)

    def squares(k, total):
        part = xv[:, pl.ds(pl.multiple_of(k * step, step), step)].astype(F32)
        return total + jnp.sum(part * part, axis=1, keepdims=True)

    total = lax.fori_loop(0, width // step, squares, jnp.zeros((128, 1), F32))
    inv = lax.rsqrt(total / width + 1e-05)
    loads[1].wait()
    loads[2].wait()
    accq[...] = jnp.zeros_like(accq)

    def project(k, _):
        part = pl.ds(pl.multiple_of(k * step, step), step)
        normed = (xv[:, part].astype(F32) * inv * gain_ref[:, part]).astype(BF16)
        accq[...] += nt(wv[:, part], normed)
        return 0

    lax.fori_loop(0, width // step, project, 0)
    cosine = rope_ref[0, i]
    sine = rope_ref[1, i]
    for b in range(9):
        front = accq[32 * b : 32 * b + 16, :]
        rear = accq[32 * b + 16 : 32 * b + 32, :]
        new_front = front * cosine - rear * sine
        new_rear = rear * cosine + front * sine
        if b < 8:
            new_front = new_front * HD ** (-0.5)
            new_rear = new_rear * HD ** (-0.5)
        qt[32 * b : 32 * b + 16, :] = new_front.astype(BF16)
        qt[32 * b + 16 : 32 * b + 32, :] = new_rear.astype(BF16)
    qt[288:320, :] = accq[288:320, :].astype(BF16)

    for third in range(3):
        for c in range(CAP):
            for gl in range(4):
                at = pl.ds((c * 4 + gl) * 128, 128)
                b = third * 4 + gl
                if b < 10:
                    spread[32 * c : 32 * c + 32, at] = qt[32 * b : 32 * b + 32, :]
                else:
                    spread[32 * c : 32 * c + 32, at] = jnp.zeros((32, 128), BF16)
        packed = nt(onehot[...], spread[...]).astype(BF16)
        sendq[:, 16 * third : 16 * third + 16, :] = packed.reshape(ng, 16, 128)

    def q_copy(k):
        there = lax.rem(g + k, ng)
        return pltpu.make_async_remote_copy(
            sendq.at[there], qx.at[i, g], qa_ssem.at[k], qa_rsem.at[k],
            device_id={"grp": there}, device_id_type=MESH)

    def q_start(k, _):
        q_copy(k).start()
        return 0

    def q_wait(k, _):
        q_copy(k).wait_recv()
        return 0

    def q_sent(k, _):
        q_copy(k).wait_send()
        return 0

    lax.fori_loop(1, ng, q_start, 0)
    qx[i, g] = sendq[g]
    lax.fori_loop(1, ng, q_wait, 0)
    q_shares = [
        pltpu.make_async_remote_copy(
            qx.at[i], qx.at[i], qg_ssem.at[o - 1], qg_rsem.at[o - 1],
            device_id={"tp": mate(t, o)}, device_id_type=MESH)
        for o in (1, 2, 3)
    ]
    for o in (2, 1, 0):
        q_shares[o].start()

    fold_row = iota(fold.shape, 0)
    fold_lane = iota(fold.shape, 1)
    fold[...] = jnp.where(
        (fold_row // 128 == fold_lane // 32) & (fold_row % 32 == fold_lane % 32), 1.0, 0.0).astype(BF16)
    row = iota((128, 128), 0)
    lane = iota((128, 128), 1)
    diagonal = jnp.where(row // 32 == lane // 32, 1.0, 0.0).astype(BF16)
    stat[...] = jnp.zeros_like(stat)

    for kind in (0, 1):
        own_cache[kind].wait()
        for o in range(3):
            cache_moves[o][kind].wait_recv()
    scf[...] = scx[...].astype(F32)
    for o in range(3):
        q_shares[o].wait_recv()

    def slots(k):
        there = lax.rem(g + k, ng)
        return there, [ids_ref[there * CAP + c] for c in range(CAP)]

    def scale_rows(n, kind, ids):
        return jnp.concatenate(
            [jnp.broadcast_to(scf[n, kind, pl.ds(ids[c], 1), :], (32, 128)) for c in range(CAP)], axis=0)

    def score(k, _):
        there, ids = slots(k)
        total = jnp.zeros((128, 128), F32)
        for n in range(4):
            q = qx[n, there, 0:32, :]
            left = jnp.concatenate([q] * CAP, axis=0) * diagonal
            keys = jnp.concatenate([kx[n, ids[c]] for c in range(CAP)], axis=0)
            total = total + nn(left, keys) * scale_rows(n, 0, ids)
        pnew[k] = jnp.full((128, 16), -jnp.inf, F32)

        @pl.when(there % 4 == i)
        def _():
            new = jnp.zeros((128, 16), F32)
            for n in range(4):
                q = qx[n, there, 0:32, :]
                left = jnp.concatenate([q] * CAP, axis=0) * diagonal
                new = new + nt(left, qx[n, there, 32:48, :])
            column = iota((128, 16), 1)
            seen = (column <= iota((128, 16), 0) % 4) & (column < 4)
            pnew[k] = jnp.where(seen, new, -jnp.inf)

        new = pnew[k]
        top = jnp.maximum(jnp.max(total, axis=1, keepdims=True), jnp.max(new, axis=1, keepdims=True))
        part = jnp.exp(total - top)
        new = jnp.exp(new - top)
        prob[k] = part
        pnew[k] = new
        mass = jnp.sum(part, axis=1, keepdims=True) + jnp.sum(new, axis=1, keepdims=True)
        stat[...] = jnp.where(lane == k, top, jnp.where(lane == ng + k, mass, stat[...]))
        return 0

    lax.fori_loop(0, ng, score, 0)

    st_send[...] = jnp.transpose(stat[...])[0 : 2 * ng, :]
    st_moves = [
        pltpu.make_async_remote_copy(
            st_send, st_recv.at[o - 1], st_ssem.at[o - 1], st_rsem.at[o - 1],
            device_id={"tp": mate(t, o)}, device_id_type=MESH)
        for o in (1, 2, 3)
    ]
    for o in (2, 1, 0):
        st_moves[o].start()
    for o in range(3):
        st_moves[o].wait_recv()
    tops = [st_send[0:ng, :]] + [st_recv[o, 0:ng, :] for o in range(3)]
    masses = [st_send[ng : 2 * ng, :]] + [st_recv[o, ng : 2 * ng, :] for o in range(3)]
    top = jnp.maximum(jnp.maximum(tops[0], tops[1]), jnp.maximum(tops[2], tops[3]))
    mass = sum(masses[o] * jnp.exp(tops[o] - top) for o in range(4))
    factor = jnp.exp(tops[0] - top) / mass
    fac[...] = jnp.transpose(jnp.concatenate([factor, jnp.zeros((128 - ng, 128), F32)], axis=0))

    own_cache[2].wait()
    for o in range(3):
        cache_moves[o][2].wait_recv()

    def head_first(q):
        at = pl.ds(q * per, per)
        return [
            pltpu.make_async_remote_copy(
                acc.at[1 - core + 2 * b, at], ra.at[b, at], ha_ssem.at[q, b], ha_rsem.at[q, b],
                device_id={"tp": mate(t, 1)}, device_id_type=MESH)
            for b in range(2)
        ]

    def head_second(q):
        at = pl.ds(q * per, per)
        return pltpu.make_async_remote_copy(
            sb.at[at], rb.at[at], hb_ssem.at[q], hb_rsem.at[q],
            device_id={"tp": mate(t, 2)}, device_id_type=MESH)

    def value(k, _):
        there, ids = slots(k)
        column = jnp.sum(jnp.where(lane == k, fac[...], 0.0), axis=1, keepdims=True)
        p = (prob[k] * column).astype(BF16).astype(F32)

        def keep(out):
            kept = jnp.zeros((32, 128), F32)
            for c in range(CAP):
                kept = kept + jnp.where(lane[0:32] // 32 == c, out[32 * c : 32 * c + 32, :], 0.0)
            return kept

        for n in range(4):
            weighted = (p * scale_rows(n, 1, ids)).astype(BF16)
            values = jnp.concatenate([vx[n, ids[c]] for c in range(CAP)], axis=0)
            acc[n, k] = keep(nt(weighted, values))

        @pl.when(there % 4 == i)
        def _():
            pn = (pnew[k] * column).astype(BF16)
            for n in range(4):
                both = qx[n, there, 32:48, :].astype(F32)
                new_values = pltpu.roll(both, 12, 0).astype(BF16)
                acc[n, k] += keep(nn(pn, new_values))

        return 0

    for q in range(chunks):
        lax.fori_loop(q * per, (q + 1) * per, value, 0)
        for copy in head_first(q):
            copy.start()
    for q in range(chunks):
        for copy in head_first(q):
            copy.wait()
        at = pl.ds(q * per, per)
        sb[at] = acc[2 * (1 - yb) + core, at] + ra[1 - yb, at]
        head_second(q).start()

    def back_copy(k):
        there = lax.rem(g + k, ng)
        return pltpu.make_async_remote_copy(
            mix.at[k], back.at[g], bk_ssem.at[k], bk_rsem.at[k],
            device_id={"grp": there}, device_id_type=MESH)

    def back_start(k, _):
        back_copy(k).start()
        return 0

    def back_wait(k, _):
        back_copy(k).wait()
        return 0

    for q in range(chunks):
        head_second(q).wait()
        at = pl.ds(q * per, per)
        mix[at] = (acc[i, at] + ra[yb, at] + rb[at]).astype(BF16)
        lax.fori_loop(max(q * per, 1), (q + 1) * per, back_start, 0)
    back[g] = mix[0]
    lax.fori_loop(1, ng, back_wait, 0)

    wide = 32 * ng
    row = iota((128, wide), 0)
    lane_w = iota((128, wide), 1)
    hit = (lane_w // 32 == col_ref[:, 0:1]) & (lane_w % 4 == row // 32)
    chosen = col_ref[:, 1:2] == lane // 32
    slots_all = back[...].reshape(wide, 128)
    mixed = jnp.zeros((128, 256), F32)
    for b in range(8):
        pick = jnp.where(hit & ((lane_w // 4) % 8 == b), 1.0, 0.0).astype(BF16)
        rows_b = jnp.where(chosen, nn(pick, slots_all), 0.0).astype(BF16)
        mixed = mixed + nn(rows_b, fold[128 * b : 128 * b + 128, :])
    mixed = mixed.astype(BF16)

    loads[3].wait()

    def columns(e, c):
        half, dy = BLOCKS[e]
        block = half * 8 + lax.rem(y + dy, 4) * 2 + c
        return pl.ds(pl.multiple_of(block * cb, 128), cb)

    def ta_copy(e):
        return pltpu.make_async_remote_copy(
            ta_send.at[e], ta_recv.at[e], ta_ssem.at[e], ta_rsem.at[e],
            device_id={"tp": mate(t, 1)}, device_id_type=MESH)

    for e in range(8):
        ta_send[e] = nn(mixed, wov[:, columns(e, 1 - core)]).astype(BF16)
        ta_copy(e).start()
    for e in range(8):
        own[e] = nn(mixed, wov[:, columns(e, core)])

    before = t + 2 * ((y + 3) % 4 - y)
    after = t + 2 * ((y + 1) % 4 - y)
    targets = (before, after, after, before, before, after)

    def tb_copy(e):
        return pltpu.make_async_remote_copy(
            tb_send.at[e], tb_recv.at[e], tb_ssem.at[e], tb_rsem.at[e],
            device_id={"tp": targets[e]}, device_id_type=MESH)

    for e in range(8):
        ta_copy(e).wait()
        summed = own[e] + ta_recv[e].astype(F32)
        if e < 4:
            tb_send[e] = summed.astype(BF16)
            tb_copy(e).start()
        elif e < 6:
            tb_copy(e - 4).wait()
            tb_send[e] = (summed + tb_recv[e - 4].astype(F32)).astype(BF16)
            tb_copy(e).start()
        else:
            fin[e - 6] = summed
    for e in (2, 3, 4, 5):
        tb_copy(e).wait()
    fin[0] = fin[0] + tb_recv[2].astype(F32) + tb_recv[4].astype(F32)
    fin[1] = fin[1] + tb_recv[3].astype(F32) + tb_recv[5].astype(F32)
    tc_send[...] = fin[1 - zh].astype(BF16)
    tc_copy = pltpu.make_async_remote_copy(
        tc_send, tc_recv, tc_ssem.at[0], tc_rsem.at[0], device_id={"tp": flip(t, 8)}, device_id_type=MESH)
    tc_copy.start()
    tc_copy.wait()
    out_ref[...] = (fin[zh] + tc_recv[...].astype(F32)).astype(BF16)

    lax.fori_loop(1, ng, q_sent, 0)
    for o in range(3):
        for kind in range(3):
            cache_moves[o][kind].wait_send()
        q_shares[o].wait_send()
        st_moves[o].wait_send()


def rope_tables(step_count, cached, particles):
    pair = np.arange(64, dtype=np.float32).reshape(4, 16)
    frequency = np.exp(-(pair / np.float32(64)) * np.log(np.float32(500000.0))).astype(np.float32)
    positions = (cached + np.arange(step_count)).astype(np.float32)
    angles = (positions[None, None, :] * frequency[:, :, None]).astype(np.float32)
    tables = np.stack([np.cos(angles), np.sin(angles)]).astype(np.float32)
    return np.repeat(tables, particles, axis=-1)


def shards(ng, inputs, norm_gain, w_query, w_keyval, w_out, kv_cache, kv_scales, ancestors):
    step_count, particles, width = inputs.shape
    cached = kv_cache.shape[3]
    my_group = lax.axis_index("grp")
    parents = ancestors.reshape(ng, particles)
    source = parents // particles
    parent_slot = parents % particles
    p_ids = jnp.arange(particles)
    caps = jnp.arange(CAP)
    wanted = source == my_group
    place = jnp.sum(wanted[:, None, :] & (p_ids[None, None, :] < p_ids[None, :, None]), axis=2)
    at_slot = wanted[:, None, :] & (place[:, None, :] == caps[None, :, None])
    ids = jnp.sum(jnp.where(at_slot, parent_slot[:, None, :], 0), axis=2).reshape(-1)
    mine = lax.dynamic_index_in_dim(source, my_group, 0, keepdims=False)
    rank = jnp.sum((mine[:, None] == mine[None, :]) & (p_ids[None, :] < p_ids[:, None]), axis=1)
    here = (mine[None, None, :] == jnp.arange(ng)[:, None, None]) & (rank[None, None, :] == caps[None, :, None])
    child = jnp.max(jnp.where(here, p_ids[None, None, :], -1), axis=2)
    child = jnp.repeat(child, 16, axis=0)
    col = jnp.tile(jnp.stack([mine, rank], axis=1), (step_count, 1))

    rope = jnp.asarray(rope_tables(step_count, cached, particles))
    rows = step_count * particles
    cb = width // lax.axis_size("tp")
    vmem = pl.BlockSpec(memory_space=pltpu.VMEM)
    smem = pl.BlockSpec(memory_space=pltpu.SMEM)
    hbm = pl.BlockSpec(memory_space=pl.ANY)
    dma = pltpu.SemaphoreType.DMA
    scratch = [
        pltpu.VMEM((rows, width), BF16),
        pltpu.VMEM((320, width), BF16),
        pltpu.VMEM((256, width), BF16),
        pltpu.VMEM((320, 128), F32),
        pltpu.VMEM((320, 128), BF16),
        pltpu.VMEM((ng * 16, 2048), BF16),
        pltpu.VMEM((128, 2048), BF16),
        pltpu.VMEM((ng, 48, 128), BF16),
        pltpu.VMEM((4, ng, 48, 128), BF16),
        pltpu.VMEM((4, particles, 32, 128), BF16),
        pltpu.VMEM((4, particles, 32, 128), BF16),
        pltpu.VMEM((4, 2, particles, 128), BF16),
        pltpu.VMEM((4, 2, particles, 128), F32),
        pltpu.VMEM((ng, 128, 128), F32),
        pltpu.VMEM((ng, 128, 16), F32),
        pltpu.VMEM((128, 128), F32),
        pltpu.VMEM((2 * ng, 128), F32),
        pltpu.VMEM((3, 2 * ng, 128), F32),
        pltpu.VMEM((128, 128), F32),
        pltpu.VMEM((4, ng, 32, 128), F32),
        pltpu.VMEM((2, ng, 32, 128), F32),
        pltpu.VMEM((ng, 32, 128), F32),
        pltpu.VMEM((ng, 32, 128), F32),
        pltpu.VMEM((ng, 32, 128), BF16),
        pltpu.VMEM((ng, 32, 128), BF16),
        pltpu.VMEM((1024, 256), BF16),
        pltpu.VMEM((8, rows, cb), BF16),
        pltpu.VMEM((8, rows, cb), BF16),
        pltpu.VMEM((8, rows, cb), F32),
        pltpu.VMEM((6, rows, cb), BF16),
        pltpu.VMEM((6, rows, cb), BF16),
        pltpu.VMEM((2, rows, cb), F32),
        pltpu.VMEM((rows, cb), BF16),
        pltpu.VMEM((rows, cb), BF16),
        dma((7,)),
        dma((3, 3)), dma((3, 3)),
        dma((ng,)), dma((ng,)),
        dma((3,)), dma((3,)),
        dma((3,)), dma((3,)),
        dma((MAX_CHUNKS, 2)), dma((MAX_CHUNKS, 2)),
        dma((MAX_CHUNKS,)), dma((MAX_CHUNKS,)),
        dma((ng,)), dma((ng,)),
        dma((8,)), dma((8,)),
        dma((6,)), dma((6,)),
        dma((1,)), dma((1,)),
    ]
    out = pl.pallas_call(
        functools.partial(kernel, ng),
        out_shape=jax.ShapeDtypeStruct((rows, cb), BF16),
        in_specs=[hbm, vmem, hbm, hbm, hbm, hbm, hbm, vmem, vmem, vmem, smem],
        out_specs=vmem,
        scratch_shapes=scratch,
        compiler_params=pltpu.CompilerParams(
            collective_id=0, has_side_effects=True, vmem_limit_bytes=52 * 1024 * 1024),
    )(
        inputs.reshape(rows, width),
        norm_gain.astype(F32).reshape(1, width),
        jnp.transpose(w_query, (1, 2, 0)).reshape(256, width),
        jnp.transpose(w_keyval, (1, 2, 0)).reshape(64, width),
        w_out.reshape(256, width),
        kv_cache,
        kv_scales.reshape(2, particles, cached),
        rope,
        child.astype(jnp.int32),
        col.astype(jnp.int32),
        ids.astype(jnp.int32),
    )
    return out.reshape(step_count, particles, cb)


def solution(mesh):
    in_specs = (
        P(None, "grp", None),
        P(),
        P(None, None, "tp"),
        P(None, None, "tp"),
        P(None, "tp", None),
        P(None, "grp", "tp", None),
        P(None, "grp", "tp", None),
        P(),
    )
    out_specs = P(None, "grp", "tp")
    return jax.shard_map(
        functools.partial(shards, mesh.shape["grp"]), mesh=mesh, in_specs=in_specs, out_specs=out_specs,
        check_vma=False)
```

time: 323 us -> 97.4 us (0.30)
  waiting for transfers between devices: 240 us -> 0 us
  Pallas kernels: 0 us -> 90.6 us
  starting transfers between devices: 19 us -> 0 us
  local copies, waits for them, and re-layouts: 22.7 us -> 4.7 us
  between operations: 13.8 us -> 0.07 us
  other arithmetic: 14.2 us -> 1.61 us
  matrix products: 12.2 us -> 0 us
    reduce_scatter x1 -> x0, waiting for transfers between devices: 119 us -> none  [shards(): lax.psum_scatter(term, 'tp', scatter_dimension=2, tiled=True)]
    pallas_call x0 -> x1, Pallas kernels: none -> 90.6 us  [shards(): pl.pallas_call(functools.partial(kernel, ng), out_shape=jax.ShapeDtypeStr...]
    all_to_all x2 -> x0, waiting for transfers between devices: 68.5 us -> none  [the longest x1 68.5 us: shards(): lax.all_to_all(outgoing[0], 'grp', split_axis=1, concat_axis=1, tiled=True)]
    ppermute x4 -> x0, waiting for transfers between devices: 52.6 us -> none  [partner_2(): return lax.ppermute(value, axis, pairs)]
    all_to_all x2 -> x0, starting transfers between devices: 16.6 us -> none  [the longest x1 8.91 us: shards(): lax.all_to_all(outgoing[1], 'grp', split_axis=1, concat_axis=1, tiled=True)]
    dot_general x7 -> x0, matrix products: 12.2 us -> none  [the longest x1 5.25 us: shards(): jnp.einsum('spd,dgf->spgf', normed, w_query, preferred_element_type=jnp.f...]
    gather x5 -> x0, local copies, waits for them, and re-layouts: 11 us -> none  [the longest x2 5.25 us: shards(): jnp.take(kv_cache, picked, axis=1)]
    all_to_all x1 -> x0, local copies, waits for them, and re-layouts: 4.75 us -> none  [shards(): lax.all_to_all(outgoing[0], 'grp', split_axis=1, concat_axis=1, tiled=True)]
  transfers between devices with their start and end apart: 7 -> 0, of which waited for: 5 -> 0; matrix products, arithmetic and copies ran while one was open for 6% -> 0% of each run, Pallas kernels for 0% -> 0%
where the time goes in v1:
time: 97.4 us; the launch traced here: 96.9 us
  Pallas kernels  90.6 us (93%)
  local copies, waits for them, and re-layouts  4.7 us (5%)
  other arithmetic  1.61 us (2%)
    pallas_call x1, Pallas kernels, shards(): pl.pallas_call(functools.partial(kernel, ng), out_shape=jax.ShapeDtypeStr...  90.6 us
    unnamed x7, local copies, waits for them, and re-layouts  3.56 us

profile of v1, /device:TPU:2, one launch (start us, length us, event | category | flops | bytes accessed | tf_op | source)
XLA Modules:
  0.0 96.9 jit_solution(5724667144595618683)
XLA Ops:
  0.0 0.8 reshape.156
  0.8 0.2 convert_reduce_fusion.1
  1.0 0.1 select_reduce_fusion.1
  1.2 0.3 convert_reduce_fusion
  1.6 0.1 select_reduce_fusion
  1.7 0.1 copy.14
  1.8 0.1 reshape.158.ids_ref
  1.9 0.1 copy.12
  2.0 0.1 copy.13
  2.1 0.7 reshape.160
  2.8 0.0 copy-start
  2.8 1.2 %copy-done = bf16[8192,2,32]{0,2,1:T(8,128)(2,1)S(1)} copy-done((bf16[8192,2,32]{0,2,1:T(8,128)(2,1)S(1)}, bf16[8192,2,32]{0,2,1:T(8,128)(2,1)}, u32[]{:S(2)}) %copy-start) | copy-done | bytes 1048600
  4.0 0.0 copy-start.1
  4.0 0.8 copy-done.1
  4.9 0.0 copy-start.2
  4.9 0.8 copy-done.2
  5.7 90.6 %shard_map.91 = bf16[128,512]{1,0:T(8,128)(2,1)S(1)} custom-call(bf16[128,8192]{1,0:T(8,128)(2,1)} %bitcast.26, f32[1,8192]{1,0:T(1,128)S(1)} %bitcast.22, bf16[256,8192]{1,0:T(8,128)(2,1)} %bitcast.24, bf16[64,8192]{1,0:T(8,128)(2,1)S(1)} %bitcast.18, bf16[256,8192]{1,0:T(8,128)(2,1)} %bitcast.25, bf16[2,32,32,512]{3,2,1,0:T(8,128)(2,1)} %kv_hbm.1, ...), custom_call_target="tpu_custom_call" | custom-call | tf_op jit(solution)/shard_map/pallas_call | solution.py:507
  96.3 0.7 copy.16
  (9 shorter events, 0.1 us)
Async XLA Ops:
  2.8 1.2 %copy-start = (bf16[8192,2,32]{0,2,1:T(8,128)(2,1)S(1)}, bf16[8192,2,32]{0,2,1:T(8,128)(2,1)}, u32[]{:S(2)}) copy-start(bf16[8192,2,32]{0,2,1:T(8,128)(2,1)} %param.12) | copy-start | bytes 3145732
  4.0 0.8 copy-start.1
  4.9 0.8 copy-start.2

commit v2 on v1

v2 whole, which is shorter than its diff:
```python
import functools

import jax
import jax.numpy as jnp
import numpy as np
from jax import lax
from jax.experimental import pallas as pl
from jax.experimental.pallas import tpu as pltpu
from jax.sharding import PartitionSpec as P

HD = 128
CAP = 4
MESH = pl.DeviceIdType.MESH
F32 = jnp.float32
BF16 = jnp.bfloat16
MAX_CHUNKS = 4
PIECES = 4
EARLY = 1
BLOCKS = ((0, 2), (1, 2), (0, 1), (1, 3), (0, 3), (1, 1), (0, 0), (1, 0))


def flip(t, bit):
    return t + bit - 2 * bit * ((t // bit) % 2)


def mate(t, offset):
    if offset & 1:
        t = flip(t, 1)
    if offset & 2:
        t = flip(t, 2)
    return t


def nt(a, b):
    return lax.dot_general(a, b, (((1,), (1,)), ((), ())), preferred_element_type=F32)


def nn(a, b):
    return jnp.dot(a, b, preferred_element_type=F32)


def iota(shape, axis):
    return lax.broadcasted_iota(jnp.int32, shape, axis)


def kernel(
    ng, x_hbm, gain_hbm, wq_hbm, wkv_hbm, wo_hbm, kv_hbm, sc_hbm, rope_hbm, anc_hbm,
    out_ref,
    xv, wv, wov, gain_v, gain_f, rope, anc, ids_v, ids_s, src_col, rank_col,
    accq, qt, onehot, spread, sendq, qx, kn, kf, vn, vf, scx, scf, prob, pb, pnew, stat, st_send, st_recv,
    fac, acc, ra, sb, rb, mix, back, fold, ta_send, ta_recv, own, tb_send, tb_recv, fin, tc_send, tc_recv,
    loc_sem, k_ssem, k_rsem, v_ssem, v_rsem, qa_ssem, qa_rsem, qg_ssem, qg_rsem, st_ssem, st_rsem, ha_ssem,
    ha_rsem, hb_ssem, hb_rsem, bk_ssem, bk_rsem, ta_ssem, ta_rsem, tb_ssem, tb_rsem, tc_ssem, tc_rsem,
):
    g = lax.axis_index("grp")
    t = lax.axis_index("tp")
    i = t % 4
    core = t % 2
    y = (t // 2) % 4
    zh = t // 8
    width = x_hbm.shape[1]
    half = out_ref.shape[1] // 2
    chunks = min(MAX_CHUNKS, ng)
    per = ng // chunks
    block_of = [mate(t, o) % 4 for o in range(4)]
    core_of = [core, 1 - core, core, 1 - core]

    loads = [
        pltpu.make_async_copy(x_hbm, xv, loc_sem.at[0]),
        pltpu.make_async_copy(wq_hbm, wv.at[pl.ds(0, 256)], loc_sem.at[1]),
        pltpu.make_async_copy(wkv_hbm, wv.at[pl.ds(256, 64)], loc_sem.at[2]),
        pltpu.make_async_copy(wo_hbm, wov, loc_sem.at[3]),
        pltpu.make_async_copy(anc_hbm, anc.at[pl.ds(0, anc_hbm.shape[0])], loc_sem.at[4]),
        pltpu.make_async_copy(gain_hbm, gain_v, loc_sem.at[5]),
        pltpu.make_async_copy(rope_hbm.at[:, i], rope, loc_sem.at[6]),
    ]
    anc[...] = jnp.full(anc.shape, -1, jnp.int32)
    for n in (4, 0, 5, 6, 1, 2):
        loads[n].start()

    barrier = pltpu.get_barrier_semaphore()
    tp_peers = [mate(t, 1), mate(t, 2), mate(t, 3), t + 2 * ((y + 3 - 2 * (y % 2)) % 4 - y), flip(t, 8)]

    def greet(k, _):
        pl.semaphore_signal(barrier, inc=1, device_id={"grp": lax.rem(g + k, ng)}, device_id_type=MESH)
        return 0

    for peer in tp_peers:
        pl.semaphore_signal(barrier, inc=1, device_id={"tp": peer}, device_id_type=MESH)
    lax.fori_loop(1, ng, greet, 0)
    pl.semaphore_wait(barrier, len(tp_peers) + ng - 1)

    def lanes_of(block):
        return pl.ds(pl.multiple_of(128 * block, 128), 128)

    def key_copies(o):
        args = dict(device_id={"tp": mate(t, o)}, device_id_type=MESH)
        lanes = lanes_of(block_of[o])
        return [
            pltpu.make_async_remote_copy(
                kv_hbm.at[0, :, :, lanes], (kn if o == 1 else kf).at[core], k_ssem.at[o - 1, 0], k_rsem.at[o - 1, 0], **args),
            pltpu.make_async_remote_copy(
                sc_hbm.at[:, :, lanes], scx.at[i], k_ssem.at[o - 1, 1], k_rsem.at[o - 1, 1], **args),
        ]

    piece = kv_hbm.shape[1] // PIECES

    def value_copy(o, j):
        at = pl.ds(j * piece, piece)
        return pltpu.make_async_remote_copy(
            kv_hbm.at[1, at, :, lanes_of(block_of[o])], (vn if o == 1 else vf).at[core, at],
            v_ssem.at[o - 1, j], v_rsem.at[o - 1, j], device_id={"tp": mate(t, o)}, device_id_type=MESH)

    key_moves = {o: key_copies(o) for o in (1, 2, 3)}
    value_moves = [value_copy(o, j) for j in range(PIECES) for o in (2, 3)]
    near_values = [value_copy(1, j) for j in range(PIECES)]
    for o in (2, 3, 1):
        key_moves[o][1].start()
    for o in (2, 3, 1):
        key_moves[o][0].start()
    for move in near_values + value_moves[:EARLY]:
        move.start()
    own_cache = [
        pltpu.make_async_copy(kv_hbm.at[0, :, :, lanes_of(i)], kn.at[core], loc_sem.at[7]),
        pltpu.make_async_copy(sc_hbm.at[:, :, lanes_of(i)], scx.at[i], loc_sem.at[8]),
        pltpu.make_async_copy(kv_hbm.at[1, :, :, lanes_of(i)], vn.at[core], loc_sem.at[9]),
    ]
    for copy in own_cache:
        copy.start()
    loads[3].start()

    row = iota((128, 128), 0)
    lane = iota((128, 128), 1)

    def ones(where):
        return jnp.where(where, 1.0, 0.0).astype(BF16)

    loads[4].wait()
    parents = anc[...]
    source = parents >> 5
    wanted = source == g
    within = iota((8, 128), 1) % 32

    def running(v):
        for shift in (1, 2, 4, 8, 16):
            v = v + jnp.where(within >= shift, pltpu.roll(v, shift, 1), 0)
        return v

    place = running(wanted.astype(jnp.int32))
    ids = jnp.zeros((8, 128), jnp.int32)
    for c in range(CAP):
        at_slot = running(jnp.where(wanted & (place == c + 1), parents & 31, 0))
        ids = jnp.where(within == 32 - CAP + c, pltpu.roll(at_slot, (c + 1 - CAP) % 128, 1), ids)
    ids_v[...] = ids
    to_scalars = pltpu.make_async_copy(ids_v, ids_s, loc_sem.at[10])
    to_scalars.start()
    mine = jnp.sum(jnp.where(iota((8, 128), 0) == g // 4, source.astype(F32), 0.0), axis=0, keepdims=True)
    mine = nn(jnp.broadcast_to(mine, (8, 128)).astype(BF16), ones(row == (g % 4) * 32 + lane % 32))[0:1]
    mine = jnp.broadcast_to(mine, (128, 128))
    mine_col = jnp.transpose(mine)
    src_col[...] = mine_col
    rank = jnp.sum(jnp.where((mine == mine_col) & (row < lane % 32), 1.0, 0.0), axis=0, keepdims=True)
    rank_col[...] = jnp.transpose(jnp.broadcast_to(rank, (128, 128)))

    slot_row = iota((ng * 16, 128), 0)
    slot_lane = iota((ng * 16, 128), 1)
    hit = (mine[0:1] == (slot_row // 16).astype(F32)) & (slot_row % 4 == slot_lane // 32)
    for c in range(CAP):
        hit_c = hit & (rank == c)
        for gl in range(4):
            onehot[:, (c * 4 + gl) * 128 : (c * 4 + gl + 1) * 128] = ones(hit_c & ((slot_row // 4) % 4 == gl))
    spread[...] = jnp.zeros_like(spread)

    loads[5].wait()
    gain_f[...] = gain_v[...].astype(F32)
    loads[0].wait()
    step = min(1024, width)

    def squares(k, total):
        part = xv[:, pl.ds(pl.multiple_of(k * step, step), step)].astype(F32)
        return total + jnp.sum(part * part, axis=1, keepdims=True)

    total = lax.fori_loop(0, width // step, squares, jnp.zeros((128, 1), F32))
    inv = lax.rsqrt(total / width + 1e-05)
    loads[1].wait()
    loads[2].wait()
    accq[...] = jnp.zeros_like(accq)

    def project(k, _):
        part = pl.ds(pl.multiple_of(k * step, step), step)
        gains = gain_f[pl.ds(pl.multiple_of(k * (step // 128), 8), step // 128), :]
        gains = jnp.concatenate([gains[r : r + 1] for r in range(step // 128)], axis=1)
        normed = (xv[:, part].astype(F32) * inv * gains).astype(BF16)
        accq[...] += nt(wv[:, part], normed)
        return 0

    lax.fori_loop(0, width // step, project, 0)
    loads[6].wait()
    cosine = rope[0]
    sine = rope[1]
    for b in range(9):
        front = accq[32 * b : 32 * b + 16, :]
        rear = accq[32 * b + 16 : 32 * b + 32, :]
        new_front = front * cosine - rear * sine
        new_rear = rear * cosine + front * sine
        if b < 8:
            new_front = new_front * HD ** (-0.5)
            new_rear = new_rear * HD ** (-0.5)
        qt[32 * b : 32 * b + 16, :] = new_front.astype(BF16)
        qt[32 * b + 16 : 32 * b + 32, :] = new_rear.astype(BF16)
    qt[288:320, :] = accq[288:320, :].astype(BF16)

    for third in range(3):
        for c in range(CAP):
            for gl in range(4):
                at = pl.ds((c * 4 + gl) * 128, 128)
                b = third * 4 + gl
                if b < 10:
                    spread[32 * c : 32 * c + 32, at] = qt[32 * b : 32 * b + 32, :]
                else:
                    spread[32 * c : 32 * c + 32, at] = jnp.zeros((32, 128), BF16)
        packed = nt(onehot[...], spread[...]).astype(BF16)
        sendq[:, 16 * third : 16 * third + 16, :] = packed.reshape(ng, 16, 128)

    def q_copy(k):
        there = lax.rem(g + k, ng)
        return pltpu.make_async_remote_copy(
            sendq.at[there], qx.at[i, g], qa_ssem.at[k], qa_rsem.at[k],
            device_id={"grp": there}, device_id_type=MESH)

    def q_share(o, k):
        here = lax.rem(g - k + ng, ng)
        return pltpu.make_async_remote_copy(
            qx.at[i, here], qx.at[i, here], qg_ssem.at[o - 1, k], qg_rsem.at[o - 1, k],
            device_id={"tp": mate(t, o)}, device_id_type=MESH)

    def q_arrival(o, k):
        here = lax.rem(g - k + ng, ng)
        return pltpu.make_async_remote_copy(
            qx.at[i, here], qx.at[block_of[o], here], qg_ssem.at[o - 1, k], qg_rsem.at[o - 1, k],
            device_id={"tp": mate(t, o)}, device_id_type=MESH)

    def q_start(k, _):
        q_copy(k).start()
        return 0

    def q_forward(k, _):
        q_copy(k).wait_recv()
        for o in (2, 3, 1):
            q_share(o, k).start()
        return 0

    lax.fori_loop(1, ng, q_start, 0)
    qx[i, g] = sendq[g]
    for o in (2, 3, 1):
        q_share(o, 0).start()
    lax.fori_loop(1, ng, q_forward, 0)
    for move in value_moves[EARLY:]:
        move.start()

    fold_row = iota(fold.shape, 0)
    fold_lane = iota(fold.shape, 1)
    fold[...] = ones((fold_row // 128 == fold_lane // 32) & (fold_row % 32 == fold_lane % 32))
    diagonal = ones(row // 32 == lane // 32)
    stat[...] = jnp.zeros_like(stat)
    to_scalars.wait()

    def slots(k):
        there = lax.rem(g - k + ng, ng)
        return there, [ids_s[there // 4, (there % 4) * 32 + 32 - CAP + c] & 31 for c in range(CAP)]

    def scale_rows(n, kind, ids):
        return jnp.concatenate(
            [jnp.broadcast_to(scf[n, kind, pl.ds(ids[c], 1), :], (32, 128)) for c in range(CAP)], axis=0)

    def queries(n, there):
        return jnp.concatenate([qx[n, there, 0:32, :]] * CAP, axis=0) * diagonal

    def block_scores(o, there, ids):
        n = block_of[o]
        held = kn if o < 2 else kf
        keys = jnp.concatenate([held[core_of[o], ids[c]] for c in range(CAP)], axis=0)
        return nn(queries(n, there), keys) * scale_rows(n, 0, ids)

    own_cache[0].wait()
    own_cache[1].wait()
    for kind in (0, 1):
        key_moves[1][kind].wait_recv()
    key_moves[2][1].wait_recv()
    key_moves[3][1].wait_recv()
    scf[...] = scx[...].astype(F32)

    def score_near(k, _):
        q_arrival(1, k).wait_recv()
        there, ids = slots(k)
        prob[k] = block_scores(0, there, ids) + block_scores(1, there, ids)
        return 0

    lax.fori_loop(0, ng, score_near, 0)
    key_moves[2][0].wait_recv()
    key_moves[3][0].wait_recv()

    def score_far(k, _):
        q_arrival(2, k).wait_recv()
        q_arrival(3, k).wait_recv()
        there, ids = slots(k)
        total = prob[k] + block_scores(2, there, ids) + block_scores(3, there, ids)
        pnew[k] = jnp.full((128, 16), -jnp.inf, F32)

        @pl.when(there % 4 == i)
        def _():
            new = jnp.zeros((128, 16), F32)
            for n in range(4):
                new = new + nt(queries(n, there), qx[n, there, 32:48, :])
            column = iota((128, 16), 1)
            seen = (column <= iota((128, 16), 0) % 4) & (column < 4)
            pnew[k] = jnp.where(seen, new, -jnp.inf)

        new = pnew[k]
        top = jnp.maximum(jnp.max(total, axis=1, keepdims=True), jnp.max(new, axis=1, keepdims=True))
        part = jnp.exp(total - top)
        new = jnp.exp(new - top)
        prob[k] = part
        pnew[k] = new
        mass = jnp.sum(part, axis=1, keepdims=True) + jnp.sum(new, axis=1, keepdims=True)
        stat[...] = jnp.where(lane == k, top, jnp.where(lane == ng + k, mass, stat[...]))
        return 0

    lax.fori_loop(0, ng, score_far, 0)

    st_send[...] = jnp.transpose(stat[...])[0 : 2 * ng, :]
    st_moves = [
        pltpu.make_async_remote_copy(
            st_send, st_recv.at[o - 1], st_ssem.at[o - 1], st_rsem.at[o - 1],
            device_id={"tp": mate(t, o)}, device_id_type=MESH)
        for o in (1, 2, 3)
    ]
    for o in (2, 1, 0):
        st_moves[o].start()
    for o in range(3):
        st_moves[o].wait_recv()
    tops = [st_send[0:ng, :]] + [st_recv[o, 0:ng, :] for o in range(3)]
    masses = [st_send[ng : 2 * ng, :]] + [st_recv[o, ng : 2 * ng, :] for o in range(3)]
    top = jnp.maximum(jnp.maximum(tops[0], tops[1]), jnp.maximum(tops[2], tops[3]))
    mass = sum(masses[o] * jnp.exp(tops[o] - top) for o in range(4))
    factor = jnp.exp(tops[0] - top) / mass
    fac[...] = jnp.transpose(jnp.concatenate([factor, jnp.zeros((128 - ng, 128), F32)], axis=0))

    def keep(out):
        kept = jnp.zeros((32, 128), F32)
        for c in range(CAP):
            kept = kept + jnp.where(lane[0:32] // 32 == c, out[32 * c : 32 * c + 32, :], 0.0)
        return kept

    def value(k, mates, first):
        there, ids = slots(k)
        if first:
            column = jnp.sum(jnp.where(lane == k, fac[...], 0.0), axis=1, keepdims=True)
            pb[k] = (prob[k] * column).astype(BF16)
            pnew[k] = pnew[k] * column
        p = pb[k].astype(F32)
        for o in mates:
            n = block_of[o]
            weighted = (p * scale_rows(n, 1, ids)).astype(BF16)
            held = vn if o < 2 else vf
            values = jnp.concatenate([held[core_of[o], ids[c]] for c in range(CAP)], axis=0)
            acc[n, k] = keep(nt(weighted, values))

        @pl.when(there % 4 == i)
        def _():
            pn = pnew[k].astype(BF16)
            for o in mates:
                n = block_of[o]
                both = qx[n, there, 32:48, :].astype(F32)
                new_values = pltpu.roll(both, 12, 0).astype(BF16)
                acc[n, k] += keep(nn(pn, new_values))

    def value_near(k, _):
        value(k, (0, 1), True)
        return 0

    def value_far(k, _):
        value(k, (2, 3), False)
        return 0

    near_sum = pltpu.make_async_remote_copy(
        acc.at[block_of[1]], ra.at[0], ha_ssem.at[0], ha_rsem.at[0],
        device_id={"tp": mate(t, 1)}, device_id_type=MESH)

    def far_sum(q):
        at = pl.ds(q * per, per)
        return pltpu.make_async_remote_copy(
            acc.at[block_of[3], at], ra.at[1, at], ha_ssem.at[1 + q], ha_rsem.at[1 + q],
            device_id={"tp": mate(t, 1)}, device_id_type=MESH)

    def chip_sum(q):
        at = pl.ds(q * per, per)
        return pltpu.make_async_remote_copy(
            sb.at[at], rb.at[at], hb_ssem.at[q], hb_rsem.at[q],
            device_id={"tp": mate(t, 2)}, device_id_type=MESH)

    def back_copy(k):
        there = lax.rem(g - k + ng, ng)
        return pltpu.make_async_remote_copy(
            mix.at[k], back.at[g], bk_ssem.at[k], bk_rsem.at[k],
            device_id={"grp": there}, device_id_type=MESH)

    def back_start(k, _):
        back_copy(k).start()
        return 0

    def back_wait(k, _):
        back_copy(k).wait()
        return 0

    def send_chip_sum(q):
        at = pl.ds(q * per, per)
        far_sum(q).wait()
        sb[at] = (acc[block_of[2], at] + ra[1, at]).astype(BF16)
        chip_sum(q).start()

    def send_back(q):
        at = pl.ds(q * per, per)
        chip_sum(q).wait()
        mix[at] = (acc[i, at] + ra[0, at] + rb[at].astype(F32)).astype(BF16)
        lax.fori_loop(max(q * per, 1), (q + 1) * per, back_start, 0)

    own_cache[2].wait()
    for move in near_values:
        move.wait_recv()
    lax.fori_loop(0, ng, value_near, 0)
    near_sum.start()
    for move in value_moves:
        move.wait_recv()
    for q in range(chunks):
        lax.fori_loop(q * per, (q + 1) * per, value_far, 0)
        far_sum(q).start()
        if q >= 1:
            send_chip_sum(q - 1)
    near_sum.wait()
    if chunks >= 2:
        send_back(0)
    send_chip_sum(chunks - 1)
    for q in range(1 if chunks >= 2 else 0, chunks):
        send_back(q)
    back[g] = mix[0]
    lax.fori_loop(1, ng, back_wait, 0)

    wide = 32 * ng
    row_w = iota((128, wide), 0)
    lane_w = iota((128, wide), 1)
    hit = ((lane_w // 32).astype(F32) == src_col[:, 0:1]) & (lane_w % 4 == row_w // 32)
    chosen = rank_col[...] == (lane // 32).astype(F32)
    slots_all = back[...].reshape(wide, 128)
    mixed = jnp.zeros((128, 256), F32)
    for b in range(8):
        pick = ones(hit & ((lane_w // 4) % 8 == b))
        rows_b = jnp.where(chosen, nn(pick, slots_all), 0.0).astype(BF16)
        mixed = mixed + nn(rows_b, fold[128 * b : 128 * b + 128, :])
    mixed = mixed.astype(BF16)

    loads[3].wait()

    def columns(h, e, c):
        part, dy = BLOCKS[e]
        block = part * 8 + lax.rem(y + dy, 4) * 2 + c
        return pl.ds(pl.multiple_of((block * 2 + h) * half, 128), half)

    def ta_copy(h, e):
        return pltpu.make_async_remote_copy(
            ta_send.at[h, e], ta_recv.at[h, e], ta_ssem.at[h, e], ta_rsem.at[h, e],
            device_id={"tp": mate(t, 1)}, device_id_type=MESH)

    before = t + 2 * ((y + 3) % 4 - y)
    after = t + 2 * ((y + 1) % 4 - y)
    targets = (before, after, after, before, before, after)

    def tb_copy(h, e):
        return pltpu.make_async_remote_copy(
            tb_send.at[h, e], tb_recv.at[h, e], tb_ssem.at[h, e], tb_rsem.at[h, e],
            device_id={"tp": targets[e]}, device_id_type=MESH)

    def tc_copy(h):
        return pltpu.make_async_remote_copy(
            tc_send.at[h], tc_recv.at[h], tc_ssem.at[h], tc_rsem.at[h],
            device_id={"tp": flip(t, 8)}, device_id_type=MESH)

    def core_sum(h, e):
        ta_copy(h, e).wait()
        return own[h, e] + ta_recv[h, e].astype(F32)

    for h in range(2):
        for e in range(8):
            ta_send[h, e] = nn(mixed, wov[:, columns(h, e, 1 - core)]).astype(BF16)
            ta_copy(h, e).start()
        for e in range(8):
            own[h, e] = nn(mixed, wov[:, columns(h, e, core)])
        for e in range(4):
            tb_send[h, e] = core_sum(h, e).astype(BF16)
            tb_copy(h, e).start()
    for h in range(2):
        for e in (4, 5):
            summed = core_sum(h, e)
            tb_copy(h, e - 4).wait()
            tb_send[h, e] = (summed + tb_recv[h, e - 4].astype(F32)).astype(BF16)
            tb_copy(h, e).start()
        fin[h, 0] = core_sum(h, 6)
        fin[h, 1] = core_sum(h, 7)
    for h in range(2):
        for e in (2, 3, 4, 5):
            tb_copy(h, e).wait()
        fin[h, 0] = fin[h, 0] + tb_recv[h, 2].astype(F32) + tb_recv[h, 4].astype(F32)
        fin[h, 1] = fin[h, 1] + tb_recv[h, 3].astype(F32) + tb_recv[h, 5].astype(F32)
        tc_send[h] = fin[h, 1 - zh].astype(BF16)
        tc_copy(h).start()
    for h in range(2):
        tc_copy(h).wait()
        out_ref[:, h * half : (h + 1) * half] = (fin[h, zh] + tc_recv[h].astype(F32)).astype(BF16)

    def q_sent(k, _):
        q_copy(k).wait_send()
        return 0

    def q_shared(k, _):
        for o in (1, 2, 3):
            q_share(o, k).wait_send()
        return 0

    lax.fori_loop(1, ng, q_sent, 0)
    lax.fori_loop(0, ng, q_shared, 0)
    for o in (1, 2, 3):
        key_moves[o][0].wait_send()
        key_moves[o][1].wait_send()
        st_moves[o - 1].wait_send()
    for move in near_values + value_moves:
        move.wait_send()


def rope_tables(step_count, cached, particles):
    pair = np.arange(64, dtype=np.float32).reshape(4, 16)
    frequency = np.exp(-(pair / np.float32(64)) * np.log(np.float32(500000.0))).astype(np.float32)
    positions = (cached + np.arange(step_count)).astype(np.float32)
    angles = (positions[None, None, :] * frequency[:, :, None]).astype(np.float32)
    tables = np.stack([np.cos(angles), np.sin(angles)]).astype(np.float32)
    return np.repeat(tables, particles, axis=-1)


def shards(ng, inputs, norm_gain, w_query, w_keyval, w_out, kv_cache, kv_scales, ancestors):
    step_count, particles, width = inputs.shape
    cached = kv_cache.shape[3]
    rope = jnp.asarray(rope_tables(step_count, cached, particles))
    missing = -ancestors.shape[0] % 128
    if missing:
        ancestors = jnp.pad(ancestors, (0, missing), constant_values=-1)
    rows = step_count * particles
    cb = width // lax.axis_size("tp")
    half = cb // 2
    vmem = pl.BlockSpec(memory_space=pltpu.VMEM)
    hbm = pl.BlockSpec(memory_space=pltpu.HBM)
    dma = pltpu.SemaphoreType.DMA
    scratch = [
        pltpu.VMEM((rows, width), BF16),
        pltpu.VMEM((320, width), BF16),
        pltpu.VMEM((256, width), BF16),
        pltpu.VMEM((width // 128, 128), BF16),
        pltpu.VMEM((width // 128, 128), F32),
        pltpu.VMEM((2, 16, 128), F32),
        pltpu.VMEM((8, 128), jnp.int32),
        pltpu.VMEM((8, 128), jnp.int32),
        pltpu.SMEM((8, 128), jnp.int32),
        pltpu.VMEM((128, 128), F32),
        pltpu.VMEM((128, 128), F32),
        pltpu.VMEM((320, 128), F32),
        pltpu.VMEM((320, 128), BF16),
        pltpu.VMEM((ng * 16, 2048), BF16),
        pltpu.VMEM((128, 2048), BF16),
        pltpu.VMEM((ng, 48, 128), BF16),
        pltpu.VMEM((4, ng, 48, 128), BF16),
        pltpu.VMEM((2, particles, 32, 128), BF16),
        pltpu.VMEM((2, particles, 32, 128), BF16),
        pltpu.VMEM((2, particles, 32, 128), BF16),
        pltpu.VMEM((2, particles, 32, 128), BF16),
        pltpu.VMEM((4, 2, particles, 128), BF16),
        pltpu.VMEM((4, 2, particles, 128), F32),
        pltpu.VMEM((ng, 128, 128), F32),
        pltpu.VMEM((ng, 128, 128), BF16),
        pltpu.VMEM((ng, 128, 16), F32),
        pltpu.VMEM((128, 128), F32),
        pltpu.VMEM((2 * ng, 128), F32),
        pltpu.VMEM((3, 2 * ng, 128), F32),
        pltpu.VMEM((128, 128), F32),
        pltpu.VMEM((4, ng, 32, 128), F32),
        pltpu.VMEM((2, ng, 32, 128), F32),
        pltpu.VMEM((ng, 32, 128), BF16),
        pltpu.VMEM((ng, 32, 128), BF16),
        pltpu.VMEM((ng, 32, 128), BF16),
        pltpu.VMEM((ng, 32, 128), BF16),
        pltpu.VMEM((1024, 256), BF16),
        pltpu.VMEM((2, 8, rows, half), BF16),
        pltpu.VMEM((2, 8, rows, half), BF16),
        pltpu.VMEM((2, 8, rows, half), F32),
        pltpu.VMEM((2, 6, rows, half), BF16),
        pltpu.VMEM((2, 6, rows, half), BF16),
        pltpu.VMEM((2, 2, rows, half), F32),
        pltpu.VMEM((2, rows, half), BF16),
        pltpu.VMEM((2, rows, half), BF16),
        dma((11,)),
        dma((3, 2)), dma((3, 2)),
        dma((3, PIECES)), dma((3, PIECES)),
        dma((ng,)), dma((ng,)),
        dma((3, ng)), dma((3, ng)),
        dma((3,)), dma((3,)),
        dma((1 + MAX_CHUNKS,)), dma((1 + MAX_CHUNKS,)),
        dma((MAX_CHUNKS,)), dma((MAX_CHUNKS,)),
        dma((ng,)), dma((ng,)),
        dma((2, 8)), dma((2, 8)),
        dma((2, 6)), dma((2, 6)),
        dma((2,)), dma((2,)),
    ]
    out = pl.pallas_call(
        functools.partial(kernel, ng),
        out_shape=jax.ShapeDtypeStruct((rows, cb), BF16),
        in_specs=[hbm] * 9,
        out_specs=vmem,
        scratch_shapes=scratch,
        compiler_params=pltpu.CompilerParams(
            collective_id=0, has_side_effects=True, vmem_limit_bytes=60 * 1024 * 1024),
    )(
        inputs.reshape(rows, width),
        norm_gain.reshape(width // 128, 128),
        jnp.transpose(w_query, (1, 2, 0)).reshape(256, width),
        jnp.transpose(w_keyval, (1, 2, 0)).reshape(64, width),
        w_out.reshape(256, width),
        kv_cache,
        kv_scales.reshape(2, particles, cached),
        rope,
        ancestors.reshape(-1, 128),
    )
    return out.reshape(step_count, particles, cb)


def solution(mesh):
    in_specs = (
        P(None, "grp", None),
        P(),
        P(None, None, "tp"),
        P(None, None, "tp"),
        P(None, "tp", None),
        P(None, "grp", "tp", None),
        P(None, "grp", "tp", None),
        P(),
    )
    out_specs = P(None, "grp", "tp")
    return jax.shard_map(
        functools.partial(shards, mesh.shape["grp"]), mesh=mesh, in_specs=in_specs, out_specs=out_specs,
        check_vma=False)
```

time: 97.4 us -> 86.2 us (0.89)
  Pallas kernels: 90.6 us -> 84.2 us
  local copies, waits for them, and re-layouts: 4.7 us -> 1.57 us
  other arithmetic: 1.61 us -> 0 us
    pallas_call x1, Pallas kernels: 90.6 us -> 84.2 us  [shards(): pl.pallas_call(functools.partial(kernel, ng), out_shape=jax.ShapeDtypeStr...]
    unnamed x7 -> x1, local copies, waits for them, and re-layouts: 3.56 us -> 1.57 us
where the time goes in v2:
time: 86.2 us; the launch traced here: 85.8 us
  Pallas kernels  84.2 us (98%)
  local copies, waits for them, and re-layouts  1.57 us (2%)
    pallas_call x1, Pallas kernels, shards(): pl.pallas_call(functools.partial(kernel, ng), out_shape=jax.ShapeDtypeStr...  84.2 us

profile of v2, /device:TPU:2, one launch (start us, length us, event | category | flops | bytes accessed | tf_op | source)
XLA Modules:
  0.0 85.8 jit_solution(4603548118173112415)
XLA Ops:
  0.0 84.2 %shard_map.91 = bf16[128,512]{1,0:T(8,128)(2,1)} custom-call(bf16[128,8192]{1,0:T(8,128)(2,1)} %bitcast.14, bf16[64,128]{1,0:T(8,128)(2,1)} %bitcast.18, bf16[256,8192]{1,0:T(8,128)(2,1)} %bitcast.12, bf16[64,8192]{1,0:T(8,128)(2,1)} %bitcast.15, bf16[256,8192]{1,0:T(8,128)(2,1)} %bitcast.13, bf16[2,32,32,512]{3,2,1,0:T(8,128)(2,1)} %kv_hbm.1, ...), custom_call_target="tpu_custom_call" | custom-call | tf_op jit(solution)/shard_map/pallas_call | solution.py:620
  84.2 1.6 %copy.11 = bf16[4,32,512]{2,1,0:T(8,128)(2,1)} copy(bf16[4,32,512]{2,1,0:T(8,128)(2,1)} %bitcast.16) | data formatting | bytes 262144

commit v3 on v2

--- a/solution.py
+++ b/solution.py
@@ -14,8 +14,8 @@
 F32 = jnp.float32
 BF16 = jnp.bfloat16
 MAX_CHUNKS = 4
-PIECES = 4
-EARLY = 1
+PIECES = 2
+EARLY = 0
 BLOCKS = ((0, 2), (1, 2), (0, 1), (1, 3), (0, 3), (1, 1), (0, 0), (1, 0))
 
 
@@ -47,7 +47,7 @@
     ng, x_hbm, gain_hbm, wq_hbm, wkv_hbm, wo_hbm, kv_hbm, sc_hbm, rope_hbm, anc_hbm,
     out_ref,
     xv, wv, wov, gain_v, gain_f, rope, anc, ids_v, ids_s, src_col, rank_col,
-    accq, qt, onehot, spread, sendq, qx, kn, kf, vn, vf, scx, scf, prob, pb, pnew, stat, st_send, st_recv,
+    accq, qt, onehot, spread, sendq, qx, kn, kf, vn, vo, vl, scx, scf, prob, pb, pnew, stat, st_send, st_recv,
     fac, acc, ra, sb, rb, mix, back, fold, ta_send, ta_recv, own, tb_send, tb_recv, fin, tc_send, tc_recv,
     loc_sem, k_ssem, k_rsem, v_ssem, v_rsem, qa_ssem, qa_rsem, qg_ssem, qg_rsem, st_ssem, st_rsem, ha_ssem,
     ha_rsem, hb_ssem, hb_rsem, bk_ssem, bk_rsem, ta_ssem, ta_rsem, tb_ssem, tb_rsem, tc_ssem, tc_rsem,
@@ -108,11 +108,11 @@
     def value_copy(o, j):
         at = pl.ds(j * piece, piece)
         return pltpu.make_async_remote_copy(
-            kv_hbm.at[1, at, :, lanes_of(block_of[o])], (vn if o == 1 else vf).at[core, at],
+            kv_hbm.at[1, at, :, lanes_of(block_of[o])], (vn.at[core, at], vl.at[at], vo.at[at])[o - 1],
             v_ssem.at[o - 1, j], v_rsem.at[o - 1, j], device_id={"tp": mate(t, o)}, device_id_type=MESH)
 
     key_moves = {o: key_copies(o) for o in (1, 2, 3)}
-    value_moves = [value_copy(o, j) for j in range(PIECES) for o in (2, 3)]
+    value_moves = [value_copy(o, j) for o in (3, 2) for j in range(PIECES)]
     near_values = [value_copy(1, j) for j in range(PIECES)]
     for o in (2, 3, 1):
         key_moves[o][1].start()
@@ -246,13 +246,23 @@
 
     def q_forward(k, _):
         q_copy(k).wait_recv()
-        for o in (2, 3, 1):
+        for o in (2, 1):
             q_share(o, k).start()
         return 0
+
+    def q_relay(k):
+        here = lax.rem(g - k + ng, ng)
+        return pltpu.make_async_remote_copy(
+            qx.at[block_of[2], here], qx.at[block_of[2], here], qg_ssem.at[2, k], qg_rsem.at[2, k],
+            device_id={"tp": mate(t, 1)}, device_id_type=MESH)
+
+    def hand_on(k):
+        q_arrival(2, k).wait_recv()
+        q_relay(k).start()
 
     lax.fori_loop(1, ng, q_start, 0)
     qx[i, g] = sendq[g]
-    for o in (2, 3, 1):
+    for o in (2, 1):
         q_share(o, 0).start()
     lax.fori_loop(1, ng, q_forward, 0)
     for move in value_moves[EARLY:]:
@@ -300,8 +310,15 @@
     key_moves[2][0].wait_recv()
     key_moves[3][0].wait_recv()
 
+    ahead = min(3, ng)
+    for k in range(ahead):
+        hand_on(k)
+
     def score_far(k, _):
-        q_arrival(2, k).wait_recv()
+        @pl.when(k + ahead < ng)
+        def _():
+            hand_on(k + ahead)
+
         q_arrival(3, k).wait_recv()
         there, ids = slots(k)
         total = prob[k] + block_scores(2, there, ids) + block_scores(3, there, ids)
@@ -362,8 +379,8 @@
         for o in mates:
             n = block_of[o]
             weighted = (p * scale_rows(n, 1, ids)).astype(BF16)
-            held = vn if o < 2 else vf
-            values = jnp.concatenate([held[core_of[o], ids[c]] for c in range(CAP)], axis=0)
+            held = [vn.at[core], vn.at[1 - core], vl, vo][o]
+            values = jnp.concatenate([held[ids[c]] for c in range(CAP)], axis=0)
             acc[n, k] = keep(nt(weighted, values))
 
         @pl.when(there % 4 == i)
@@ -379,8 +396,12 @@
         value(k, (0, 1), True)
         return 0
 
-    def value_far(k, _):
-        value(k, (2, 3), False)
+    def value_other(k, _):
+        value(k, (3,), False)
+        return 0
+
+    def value_last(k, _):
+        value(k, (2,), False)
         return 0
 
     near_sum = pltpu.make_async_remote_copy(
@@ -430,19 +451,21 @@
         move.wait_recv()
     lax.fori_loop(0, ng, value_near, 0)
     near_sum.start()
-    for move in value_moves:
+    for move in value_moves[:PIECES]:
         move.wait_recv()
     for q in range(chunks):
-        lax.fori_loop(q * per, (q + 1) * per, value_far, 0)
+        lax.fori_loop(q * per, (q + 1) * per, value_other, 0)
         far_sum(q).start()
-        if q >= 1:
-            send_chip_sum(q - 1)
-    near_sum.wait()
-    if chunks >= 2:
-        send_back(0)
-    send_chip_sum(chunks - 1)
-    for q in range(1 if chunks >= 2 else 0, chunks):
-        send_back(q)
+    for move in value_moves[PIECES:]:
+        move.wait_recv()
+    for q in range(chunks):
+        lax.fori_loop(q * per, (q + 1) * per, value_last, 0)
+        send_chip_sum(q)
+        if q == 0:
+            near_sum.wait()
+        else:
+            send_back(q - 1)
+    send_back(chunks - 1)
     back[g] = mix[0]
     lax.fori_loop(1, ng, back_wait, 0)
 
@@ -489,23 +512,31 @@
         ta_copy(h, e).wait()
         return own[h, e] + ta_recv[h, e].astype(F32)
 
-    for h in range(2):
-        for e in range(8):
+    def first_step(h, pair):
+        for e in pair:
             ta_send[h, e] = nn(mixed, wov[:, columns(h, e, 1 - core)]).astype(BF16)
             ta_copy(h, e).start()
-        for e in range(8):
+        for e in pair:
             own[h, e] = nn(mixed, wov[:, columns(h, e, core)])
-        for e in range(4):
-            tb_send[h, e] = core_sum(h, e).astype(BF16)
-            tb_copy(h, e).start()
-    for h in range(2):
-        for e in (4, 5):
+
+    def second_step(h, pair):
+        for e in pair:
             summed = core_sum(h, e)
-            tb_copy(h, e - 4).wait()
-            tb_send[h, e] = (summed + tb_recv[h, e - 4].astype(F32)).astype(BF16)
-            tb_copy(h, e).start()
-        fin[h, 0] = core_sum(h, 6)
-        fin[h, 1] = core_sum(h, 7)
+            if e in (4, 5):
+                tb_copy(h, e - 4).wait()
+                summed = summed + tb_recv[h, e - 4].astype(F32)
+            if e < 6:
+                tb_send[h, e] = summed.astype(BF16)
+                tb_copy(h, e).start()
+            else:
+                fin[h, e - 6] = summed
+
+    order = [(0, (0, 1)), (0, (2, 3)), (1, (0, 1)), (0, (4, 5)), (1, (2, 3)), (1, (4, 5)), (0, (6, 7)), (1, (6, 7))]
+    for at, step_at in enumerate(order):
+        first_step(*step_at)
+        if at:
+            second_step(*order[at - 1])
+    second_step(*order[-1])
     for h in range(2):
         for e in (2, 3, 4, 5):
             tb_copy(h, e).wait()
@@ -522,8 +553,9 @@
         return 0
 
     def q_shared(k, _):
-        for o in (1, 2, 3):
+        for o in (1, 2):
             q_share(o, k).wait_send()
+        q_relay(k).wait_send()
         return 0
 
     lax.fori_loop(1, ng, q_sent, 0)
@@ -579,7 +611,8 @@
         pltpu.VMEM((2, particles, 32, 128), BF16),
         pltpu.VMEM((2, particles, 32, 128), BF16),
         pltpu.VMEM((2, particles, 32, 128), BF16),
-        pltpu.VMEM((2, particles, 32, 128), BF16),
+        pltpu.VMEM((particles, 32, 128), BF16),
+        pltpu.VMEM((particles, 32, 128), BF16),
         pltpu.VMEM((4, 2, particles, 128), BF16),
         pltpu.VMEM((4, 2, particles, 128), F32),
         pltpu.VMEM((ng, 128, 128), F32),

time: 86.2 us -> 86.6 us (level); the launches traced: 85.8 us -> 85 us
  no operation moved by 1% of the time
where the time goes in v3:
time: 86.6 us; the launch traced here: 85 us
  Pallas kernels  83.4 us (96%)
  local copies, waits for them, and re-layouts  1.57 us (2%)
    pallas_call x1, Pallas kernels, shards(): pl.pallas_call(functools.partial(kernel, ng), out_shape=jax.ShapeDtypeStr...  83.4 us

profile of v3, /device:TPU:2, one launch (start us, length us, event | category | flops | bytes accessed | tf_op | source)
XLA Modules:
  0.0 85.0 jit_solution(3368238110012772453)
XLA Ops:
  0.0 83.4 %shard_map.91 = bf16[128,512]{1,0:T(8,128)(2,1)} custom-call(bf16[128,8192]{1,0:T(8,128)(2,1)} %bitcast.14, bf16[64,128]{1,0:T(8,128)(2,1)} %bitcast.18, bf16[256,8192]{1,0:T(8,128)(2,1)} %bitcast.12, bf16[64,8192]{1,0:T(8,128)(2,1)} %bitcast.15, bf16[256,8192]{1,0:T(8,128)(2,1)} %bitcast.13, bf16[2,32,32,512]{3,2,1,0:T(8,128)(2,1)} %kv_hbm.1, ...), custom_call_target="tpu_custom_call" | custom-call | tf_op jit(solution)/shard_map/pallas_call | solution.py:653
  83.4 1.6 %copy.11 = bf16[4,32,512]{2,1,0:T(8,128)(2,1)} copy(bf16[4,32,512]{2,1,0:T(8,128)(2,1)} %bitcast.16) | data formatting | bytes 262144

commit v4 on v3

--- a/solution.py
+++ b/solution.py
@@ -15,7 +15,7 @@
 BF16 = jnp.bfloat16
 MAX_CHUNKS = 4
 PIECES = 2
-EARLY = 0
+EARLY = 1
 BLOCKS = ((0, 2), (1, 2), (0, 1), (1, 3), (0, 3), (1, 1), (0, 0), (1, 0))
 
 
@@ -118,7 +118,7 @@
         key_moves[o][1].start()
     for o in (2, 3, 1):
         key_moves[o][0].start()
-    for move in near_values + value_moves[:EARLY]:
+    for move in near_values:
         move.start()
     own_cache = [
         pltpu.make_async_copy(kv_hbm.at[0, :, :, lanes_of(i)], kn.at[core], loc_sem.at[7]),
@@ -265,7 +265,7 @@
     for o in (2, 1):
         q_share(o, 0).start()
     lax.fori_loop(1, ng, q_forward, 0)
-    for move in value_moves[EARLY:]:
+    for move in value_moves[:EARLY]:
         move.start()
 
     fold_row = iota(fold.shape, 0)
@@ -300,50 +300,78 @@
     key_moves[3][1].wait_recv()
     scf[...] = scx[...].astype(F32)
 
-    def score_near(k, _):
-        q_arrival(1, k).wait_recv()
-        there, ids = slots(k)
-        prob[k] = block_scores(0, there, ids) + block_scores(1, there, ids)
-        return 0
-
-    lax.fori_loop(0, ng, score_near, 0)
+    def each(first, last, width, body):
+        width = min(width, last - first)
+
+        def run(j, _):
+            body([first + j * width + d for d in range(width)])
+            return 0
+
+        lax.fori_loop(0, (last - first) // width, run, 0)
+
+    def score_near(ks):
+        for k in ks:
+            q_arrival(1, k).wait_recv()
+        totals = []
+        for k in ks:
+            there, ids = slots(k)
+            totals.append(block_scores(0, there, ids) + block_scores(1, there, ids))
+        for k, total in zip(ks, totals):
+            prob[k] = total
+
+    each(0, ng, 2, score_near)
+
+    def hand_all(k, _):
+        hand_on(k)
+        return 0
+
+    lax.fori_loop(0, ng, hand_all, 0)
     key_moves[2][0].wait_recv()
     key_moves[3][0].wait_recv()
-
-    ahead = min(3, ng)
-    for k in range(ahead):
-        hand_on(k)
-
-    def score_far(k, _):
-        @pl.when(k + ahead < ng)
-        def _():
-            hand_on(k + ahead)
-
+    pnew[...] = jnp.full(pnew.shape, -jnp.inf, F32)
+
+    def far_arrival(k, _):
         q_arrival(3, k).wait_recv()
-        there, ids = slots(k)
-        total = prob[k] + block_scores(2, there, ids) + block_scores(3, there, ids)
-        pnew[k] = jnp.full((128, 16), -jnp.inf, F32)
-
-        @pl.when(there % 4 == i)
-        def _():
-            new = jnp.zeros((128, 16), F32)
-            for n in range(4):
-                new = new + nt(queries(n, there), qx[n, there, 32:48, :])
-            column = iota((128, 16), 1)
-            seen = (column <= iota((128, 16), 0) % 4) & (column < 4)
-            pnew[k] = jnp.where(seen, new, -jnp.inf)
-
-        new = pnew[k]
-        top = jnp.maximum(jnp.max(total, axis=1, keepdims=True), jnp.max(new, axis=1, keepdims=True))
-        part = jnp.exp(total - top)
-        new = jnp.exp(new - top)
-        prob[k] = part
-        pnew[k] = new
-        mass = jnp.sum(part, axis=1, keepdims=True) + jnp.sum(new, axis=1, keepdims=True)
-        stat[...] = jnp.where(lane == k, top, jnp.where(lane == ng + k, mass, stat[...]))
-        return 0
-
-    lax.fori_loop(0, ng, score_far, 0)
+        return 0
+
+    lax.fori_loop(0, ng, far_arrival, 0)
+    first_new = (g - i + 4 * ng) % 4
+    share = max(ng // 4, 1)
+
+    def score_new(j, _):
+        k = lax.rem(first_new + 4 * j, ng)
+        there, _ = slots(k)
+        new = jnp.zeros((128, 16), F32)
+        for n in range(4):
+            new = new + nt(queries(n, there), qx[n, there, 32:48, :])
+        column = iota((128, 16), 1)
+        seen = (column <= iota((128, 16), 0) % 4) & (column < 4)
+        if ng < 4:
+            seen = seen & (there == i)
+        pnew[k] = jnp.where(seen, new, -jnp.inf)
+        return 0
+
+    lax.fori_loop(0, share, score_new, 0)
+
+    def score_far(ks):
+        done = []
+        for k in ks:
+            there, ids = slots(k)
+            total = prob[k] + block_scores(2, there, ids) + block_scores(3, there, ids)
+            new = pnew[k]
+            top = jnp.maximum(jnp.max(total, axis=1, keepdims=True), jnp.max(new, axis=1, keepdims=True))
+            part = jnp.exp(total - top)
+            new = jnp.exp(new - top)
+            mass = jnp.sum(part, axis=1, keepdims=True) + jnp.sum(new, axis=1, keepdims=True)
+            done.append((part, new, top, mass))
+        both = stat[...]
+        for k, (part, new, top, mass) in zip(ks, done):
+            prob[k] = part
+            pnew[k] = new
+            both = jnp.where(lane == k, top, jnp.where(lane == ng + k, mass, both))
+        stat[...] = both
+
+    each(0, ng, 2, score_far)
 
     st_send[...] = jnp.transpose(stat[...])[0 : 2 * ng, :]
     st_moves = [
@@ -354,6 +382,8 @@
     ]
     for o in (2, 1, 0):
         st_moves[o].start()
+    for move in value_moves[EARLY:]:
+        move.start()
     for o in range(3):
         st_moves[o].wait_recv()
     tops = [st_send[0:ng, :]] + [st_recv[o, 0:ng, :] for o in range(3)]
@@ -369,39 +399,37 @@
             kept = kept + jnp.where(lane[0:32] // 32 == c, out[32 * c : 32 * c + 32, :], 0.0)
         return kept
 
-    def value(k, mates, first):
-        there, ids = slots(k)
+    def value(ks, mates, first):
         if first:
-            column = jnp.sum(jnp.where(lane == k, fac[...], 0.0), axis=1, keepdims=True)
-            pb[k] = (prob[k] * column).astype(BF16)
-            pnew[k] = pnew[k] * column
-        p = pb[k].astype(F32)
-        for o in mates:
-            n = block_of[o]
-            weighted = (p * scale_rows(n, 1, ids)).astype(BF16)
-            held = [vn.at[core], vn.at[1 - core], vl, vo][o]
-            values = jnp.concatenate([held[ids[c]] for c in range(CAP)], axis=0)
-            acc[n, k] = keep(nt(weighted, values))
-
-        @pl.when(there % 4 == i)
-        def _():
-            pn = pnew[k].astype(BF16)
+            for k in ks:
+                column = jnp.sum(jnp.where(lane == k, fac[...], 0.0), axis=1, keepdims=True)
+                pb[k] = (prob[k] * column).astype(BF16)
+        kept = []
+        for k in ks:
+            there, ids = slots(k)
+            p = pb[k].astype(F32)
             for o in mates:
-                n = block_of[o]
-                both = qx[n, there, 32:48, :].astype(F32)
-                new_values = pltpu.roll(both, 12, 0).astype(BF16)
-                acc[n, k] += keep(nn(pn, new_values))
-
-    def value_near(k, _):
-        value(k, (0, 1), True)
-        return 0
-
-    def value_other(k, _):
-        value(k, (3,), False)
-        return 0
-
-    def value_last(k, _):
-        value(k, (2,), False)
+                weighted = (p * scale_rows(block_of[o], 1, ids)).astype(BF16)
+                held = [vn.at[core], vn.at[1 - core], vl, vo][o]
+                values = jnp.concatenate([held[ids[c]] for c in range(CAP)], axis=0)
+                kept.append((block_of[o], k, keep(nt(weighted, values))))
+        for n, k, out in kept:
+            acc[n, k] = acc[n, k] + out
+
+    def value_new(j, _):
+        k = lax.rem(first_new + 4 * j, ng)
+        there, _ = slots(k)
+        pn = pnew[k].astype(BF16)
+        for n in range(4):
+            both = qx[n, there, 32:48, :].astype(F32)
+            new_values = pltpu.roll(both, 12, 0).astype(BF16)
+            acc[n, k] = keep(nn(pn, new_values))
+        return 0
+
+    def scale_new(j, _):
+        k = lax.rem(first_new + 4 * j, ng)
+        column = jnp.sum(jnp.where(lane == k, fac[...], 0.0), axis=1, keepdims=True)
+        pnew[k] = pnew[k] * column
         return 0
 
     near_sum = pltpu.make_async_remote_copy(
@@ -446,20 +474,23 @@
         mix[at] = (acc[i, at] + ra[0, at] + rb[at].astype(F32)).astype(BF16)
         lax.fori_loop(max(q * per, 1), (q + 1) * per, back_start, 0)
 
+    acc[...] = jnp.zeros_like(acc)
+    lax.fori_loop(0, share, scale_new, 0)
+    lax.fori_loop(0, share, value_new, 0)
     own_cache[2].wait()
     for move in near_values:
         move.wait_recv()
-    lax.fori_loop(0, ng, value_near, 0)
+    each(0, ng, 2, lambda ks: value(ks, (0, 1), True))
     near_sum.start()
     for move in value_moves[:PIECES]:
         move.wait_recv()
     for q in range(chunks):
-        lax.fori_loop(q * per, (q + 1) * per, value_other, 0)
+        each(q * per, (q + 1) * per, 4, lambda ks: value(ks, (3,), False))
         far_sum(q).start()
     for move in value_moves[PIECES:]:
         move.wait_recv()
     for q in range(chunks):
-        lax.fori_loop(q * per, (q + 1) * per, value_last, 0)
+        each(q * per, (q + 1) * per, 4, lambda ks: value(ks, (2,), False))
         send_chip_sum(q)
         if q == 0:
             near_sum.wait()
@@ -531,19 +562,33 @@
             else:
                 fin[h, e - 6] = summed
 
-    order = [(0, (0, 1)), (0, (2, 3)), (1, (0, 1)), (0, (4, 5)), (1, (2, 3)), (1, (4, 5)), (0, (6, 7)), (1, (6, 7))]
-    for at, step_at in enumerate(order):
-        first_step(*step_at)
-        if at:
-            second_step(*order[at - 1])
-    second_step(*order[-1])
-    for h in range(2):
+    def last_step(h):
         for e in (2, 3, 4, 5):
             tb_copy(h, e).wait()
         fin[h, 0] = fin[h, 0] + tb_recv[h, 2].astype(F32) + tb_recv[h, 4].astype(F32)
         fin[h, 1] = fin[h, 1] + tb_recv[h, 3].astype(F32) + tb_recv[h, 5].astype(F32)
         tc_send[h] = fin[h, 1 - zh].astype(BF16)
         tc_copy(h).start()
+
+    opposite, direct, joined, kept = (0, 1), (2, 3), (4, 5), (6, 7)
+    first_step(0, opposite)
+    first_step(0, direct)
+    second_step(0, opposite)
+    first_step(1, opposite)
+    second_step(0, direct)
+    first_step(0, joined)
+    second_step(1, opposite)
+    first_step(1, direct)
+    second_step(0, joined)
+    first_step(1, joined)
+    second_step(1, direct)
+    first_step(0, kept)
+    first_step(1, kept)
+    second_step(0, kept)
+    second_step(1, joined)
+    last_step(0)
+    second_step(1, kept)
+    last_step(1)
     for h in range(2):
         tc_copy(h).wait()
         out_ref[:, h * half : (h + 1) * half] = (fin[h, zh] + tc_recv[h].astype(F32)).astype(BF16)

time: 86.6 us -> 80.6 us (0.931)
  Pallas kernels: 83.4 us -> 78.3 us
    pallas_call x1, Pallas kernels: 83.4 us -> 78.3 us  [shards(): pl.pallas_call(functools.partial(kernel, ng), out_shape=jax.ShapeDtypeStr...]
where the time goes in v4:
time: 80.6 us; the launch traced here: 79.8 us
  Pallas kernels  78.3 us (97%)
  local copies, waits for them, and re-layouts  1.57 us (2%)
    pallas_call x1, Pallas kernels, shards(): pl.pallas_call(functools.partial(kernel, ng), out_shape=jax.ShapeDtypeStr...  78.3 us

profile of v4, /device:TPU:2, one launch (start us, length us, event | category | flops | bytes accessed | tf_op | source)
XLA Modules:
  0.0 79.8 jit_solution(10454877250882025766)
XLA Ops:
  0.0 78.3 %shard_map.91 = bf16[128,512]{1,0:T(8,128)(2,1)} custom-call(bf16[128,8192]{1,0:T(8,128)(2,1)} %bitcast.14, bf16[64,128]{1,0:T(8,128)(2,1)} %bitcast.18, bf16[256,8192]{1,0:T(8,128)(2,1)} %bitcast.12, bf16[64,8192]{1,0:T(8,128)(2,1)} %bitcast.15, bf16[256,8192]{1,0:T(8,128)(2,1)} %bitcast.13, bf16[2,32,32,512]{3,2,1,0:T(8,128)(2,1)} %kv_hbm.1, ...), custom_call_target="tpu_custom_call" | custom-call | tf_op jit(solution)/shard_map/pallas_call | solution.py:698
  78.3 1.6 %copy.11 = bf16[4,32,512]{2,1,0:T(8,128)(2,1)} copy(bf16[4,32,512]{2,1,0:T(8,128)(2,1)} %bitcast.16) | data formatting | bytes 262144

commit v5 on v4

--- a/solution.py
+++ b/solution.py
@@ -14,8 +14,8 @@
 F32 = jnp.float32
 BF16 = jnp.bfloat16
 MAX_CHUNKS = 4
-PIECES = 2
-EARLY = 1
+PIECES = 4
+EARLY = 5
 BLOCKS = ((0, 2), (1, 2), (0, 1), (1, 3), (0, 3), (1, 1), (0, 0), (1, 0))
 
 
@@ -492,11 +492,9 @@
     for q in range(chunks):
         each(q * per, (q + 1) * per, 4, lambda ks: value(ks, (2,), False))
         send_chip_sum(q)
-        if q == 0:
-            near_sum.wait()
-        else:
-            send_back(q - 1)
-    send_back(chunks - 1)
+    near_sum.wait()
+    for q in range(chunks):
+        send_back(q)
     back[g] = mix[0]
     lax.fori_loop(1, ng, back_wait, 0)
 
@@ -529,19 +527,17 @@
     after = t + 2 * ((y + 1) % 4 - y)
     targets = (before, after, after, before, before, after)
 
-    def tb_copy(h, e):
-        return pltpu.make_async_remote_copy(
-            tb_send.at[h, e], tb_recv.at[h, e], tb_ssem.at[h, e], tb_rsem.at[h, e],
+    def tb_copy(u, e):
+        return pltpu.make_async_remote_copy(
+            tb_send.at[u, e], tb_recv.at[u, e], tb_ssem.at[u, e], tb_rsem.at[u, e],
             device_id={"tp": targets[e]}, device_id_type=MESH)
 
-    def tc_copy(h):
-        return pltpu.make_async_remote_copy(
-            tc_send.at[h], tc_recv.at[h], tc_ssem.at[h], tc_rsem.at[h],
+    def tc_copy(u):
+        return pltpu.make_async_remote_copy(
+            tc_send.at[u], tc_recv.at[u], tc_ssem.at[u], tc_rsem.at[u],
             device_id={"tp": flip(t, 8)}, device_id_type=MESH)
 
-    def core_sum(h, e):
-        ta_copy(h, e).wait()
-        return own[h, e] + ta_recv[h, e].astype(F32)
+    quarter = half // 2
 
     def first_step(h, pair):
         for e in pair:
@@ -550,48 +546,58 @@
         for e in pair:
             own[h, e] = nn(mixed, wov[:, columns(h, e, core)])
 
-    def second_step(h, pair):
+    def second_step(u, pair):
+        h, at = u // 2, pl.ds((u % 2) * quarter, quarter)
         for e in pair:
-            summed = core_sum(h, e)
+            if u % 2 == 0:
+                ta_copy(h, e).wait()
+            summed = own[h, e, :, at] + ta_recv[h, e, :, at].astype(F32)
             if e in (4, 5):
-                tb_copy(h, e - 4).wait()
-                summed = summed + tb_recv[h, e - 4].astype(F32)
+                tb_copy(u, e - 4).wait()
+                summed = summed + tb_recv[u, e - 4].astype(F32)
             if e < 6:
-                tb_send[h, e] = summed.astype(BF16)
-                tb_copy(h, e).start()
+                tb_send[u, e] = summed.astype(BF16)
+                tb_copy(u, e).start()
             else:
-                fin[h, e - 6] = summed
-
-    def last_step(h):
+                fin[u, e - 6] = summed
+
+    def last_step(u):
+        second_step(u, kept)
         for e in (2, 3, 4, 5):
-            tb_copy(h, e).wait()
-        fin[h, 0] = fin[h, 0] + tb_recv[h, 2].astype(F32) + tb_recv[h, 4].astype(F32)
-        fin[h, 1] = fin[h, 1] + tb_recv[h, 3].astype(F32) + tb_recv[h, 5].astype(F32)
-        tc_send[h] = fin[h, 1 - zh].astype(BF16)
-        tc_copy(h).start()
+            tb_copy(u, e).wait()
+        fin[u, 0] = fin[u, 0] + tb_recv[u, 2].astype(F32) + tb_recv[u, 4].astype(F32)
+        fin[u, 1] = fin[u, 1] + tb_recv[u, 3].astype(F32) + tb_recv[u, 5].astype(F32)
+        tc_send[u] = fin[u, 1 - zh].astype(BF16)
+        tc_copy(u).start()
 
     opposite, direct, joined, kept = (0, 1), (2, 3), (4, 5), (6, 7)
     first_step(0, opposite)
     first_step(0, direct)
     second_step(0, opposite)
+    second_step(1, opposite)
+    first_step(0, joined)
+    second_step(0, direct)
     first_step(1, opposite)
-    second_step(0, direct)
-    first_step(0, joined)
-    second_step(1, opposite)
+    second_step(0, joined)
+    second_step(1, direct)
+    second_step(1, joined)
     first_step(1, direct)
-    second_step(0, joined)
+    second_step(2, opposite)
+    second_step(3, opposite)
     first_step(1, joined)
-    second_step(1, direct)
+    second_step(2, direct)
     first_step(0, kept)
+    second_step(2, joined)
+    second_step(3, direct)
+    last_step(0)
     first_step(1, kept)
-    second_step(0, kept)
-    second_step(1, joined)
-    last_step(0)
-    second_step(1, kept)
+    second_step(3, joined)
     last_step(1)
-    for h in range(2):
-        tc_copy(h).wait()
-        out_ref[:, h * half : (h + 1) * half] = (fin[h, zh] + tc_recv[h].astype(F32)).astype(BF16)
+    last_step(2)
+    last_step(3)
+    for u in range(4):
+        tc_copy(u).wait()
+        out_ref[:, u * quarter : (u + 1) * quarter] = (fin[u, zh] + tc_recv[u].astype(F32)).astype(BF16)
 
     def q_sent(k, _):
         q_copy(k).wait_send()
@@ -677,11 +683,11 @@
         pltpu.VMEM((2, 8, rows, half), BF16),
         pltpu.VMEM((2, 8, rows, half), BF16),
         pltpu.VMEM((2, 8, rows, half), F32),
-        pltpu.VMEM((2, 6, rows, half), BF16),
-        pltpu.VMEM((2, 6, rows, half), BF16),
-        pltpu.VMEM((2, 2, rows, half), F32),
-        pltpu.VMEM((2, rows, half), BF16),
-        pltpu.VMEM((2, rows, half), BF16),
+        pltpu.VMEM((4, 6, rows, half // 2), BF16),
+        pltpu.VMEM((4, 6, rows, half // 2), BF16),
+        pltpu.VMEM((4, 2, rows, half // 2), F32),
+        pltpu.VMEM((4, rows, half // 2), BF16),
+        pltpu.VMEM((4, rows, half // 2), BF16),
         dma((11,)),
         dma((3, 2)), dma((3, 2)),
         dma((3, PIECES)), dma((3, PIECES)),
@@ -692,8 +698,8 @@
         dma((MAX_CHUNKS,)), dma((MAX_CHUNKS,)),
         dma((ng,)), dma((ng,)),
         dma((2, 8)), dma((2, 8)),
-        dma((2, 6)), dma((2, 6)),
-        dma((2,)), dma((2,)),
+        dma((4, 6)), dma((4, 6)),
+        dma((4,)), dma((4,)),
     ]
     out = pl.pallas_call(
         functools.partial(kernel, ng),

time: 80.6 us -> 75.5 us (0.937)
  Pallas kernels: 78.3 us -> 73.6 us
    pallas_call x1, Pallas kernels: 78.3 us -> 73.6 us  [shards(): pl.pallas_call(functools.partial(kernel, ng), out_shape=jax.ShapeDtypeStr...]
where the time goes in v5:
time: 75.5 us; the launch traced here: 75.2 us
  Pallas kernels  73.6 us (97%)
  local copies, waits for them, and re-layouts  1.57 us (2%)
    pallas_call x1, Pallas kernels, shards(): pl.pallas_call(functools.partial(kernel, ng), out_shape=jax.ShapeDtypeStr...  73.6 us
    unnamed x1, local copies, waits for them, and re-layouts  1.57 us

profile of v5, /device:TPU:2, one launch (start us, length us, event | category | flops | bytes accessed | tf_op | source)
XLA Modules:
  0.0 75.2 jit_solution(4047502294882621576)
XLA Ops:
  0.0 73.6 %shard_map.91 = bf16[128,512]{1,0:T(8,128)(2,1)} custom-call(bf16[128,8192]{1,0:T(8,128)(2,1)} %bitcast.14, bf16[64,128]{1,0:T(8,128)(2,1)} %bitcast.18, bf16[256,8192]{1,0:T(8,128)(2,1)} %bitcast.12, bf16[64,8192]{1,0:T(8,128)(2,1)} %bitcast.15, bf16[256,8192]{1,0:T(8,128)(2,1)} %bitcast.13, bf16[2,32,32,512]{3,2,1,0:T(8,128)(2,1)} %kv_hbm.1, ...), custom_call_target="tpu_custom_call" | custom-call | tf_op jit(solution)/shard_map/pallas_call | solution.py:704
  73.6 1.6 %copy.11 = bf16[4,32,512]{2,1,0:T(8,128)(2,1)} copy(bf16[4,32,512]{2,1,0:T(8,128)(2,1)} %bitcast.16) | data formatting | bytes 262144

commit v6 on v5

--- a/solution.py
+++ b/solution.py
@@ -15,7 +15,6 @@
 BF16 = jnp.bfloat16
 MAX_CHUNKS = 4
 PIECES = 4
-EARLY = 5
 BLOCKS = ((0, 2), (1, 2), (0, 1), (1, 3), (0, 3), (1, 1), (0, 0), (1, 0))
 
 
@@ -47,10 +46,10 @@
     ng, x_hbm, gain_hbm, wq_hbm, wkv_hbm, wo_hbm, kv_hbm, sc_hbm, rope_hbm, anc_hbm,
     out_ref,
     xv, wv, wov, gain_v, gain_f, rope, anc, ids_v, ids_s, src_col, rank_col,
-    accq, qt, onehot, spread, sendq, qx, kn, kf, vn, vo, vl, scx, scf, prob, pb, pnew, stat, st_send, st_recv,
-    fac, acc, ra, sb, rb, mix, back, fold, ta_send, ta_recv, own, tb_send, tb_recv, fin, tc_send, tc_recv,
-    loc_sem, k_ssem, k_rsem, v_ssem, v_rsem, qa_ssem, qa_rsem, qg_ssem, qg_rsem, st_ssem, st_rsem, ha_ssem,
-    ha_rsem, hb_ssem, hb_rsem, bk_ssem, bk_rsem, ta_ssem, ta_rsem, tb_ssem, tb_rsem, tc_ssem, tc_rsem,
+    accq, qt, onehot, spread, sendq, qx, kn, kf, vown, sv, svf, scx, scf, prob, px, pnp, pnew, stat, st_send, st_recv,
+    facn, fac, mix, back, picks, fold, ta_send, ta_recv, own, tb_send, tb_recv, fin, tc_send, tc_recv,
+    loc_sem, k_ssem, k_rsem, p_ssem, p_rsem, pn_ssem, pn_rsem, qa_ssem, qa_rsem, qg_ssem, qg_rsem, st_ssem, st_rsem,
+    bk_ssem, bk_rsem, ta_ssem, ta_rsem, tb_ssem, tb_rsem, tc_ssem, tc_rsem,
 ):
     g = lax.axis_index("grp")
     t = lax.axis_index("tp")
@@ -96,35 +95,33 @@
     def key_copies(o):
         args = dict(device_id={"tp": mate(t, o)}, device_id_type=MESH)
         lanes = lanes_of(block_of[o])
+        piece = kv_hbm.shape[1] // PIECES
+        pieces = [pl.ds(j * piece, piece) for j in range(PIECES)]
+        held = kn if o == 1 else kf
         return [
             pltpu.make_async_remote_copy(
-                kv_hbm.at[0, :, :, lanes], (kn if o == 1 else kf).at[core], k_ssem.at[o - 1, 0], k_rsem.at[o - 1, 0], **args),
+                kv_hbm.at[0, at, :, lanes], held.at[core, at], k_ssem.at[o - 1, j], k_rsem.at[o - 1, j], **args)
+            for j, at in enumerate(pieces)
+        ] + [
             pltpu.make_async_remote_copy(
-                sc_hbm.at[:, :, lanes], scx.at[i], k_ssem.at[o - 1, 1], k_rsem.at[o - 1, 1], **args),
+                sc_hbm.at[:, :, lanes], scx.at[i], k_ssem.at[o - 1, PIECES], k_rsem.at[o - 1, PIECES], **args),
         ]
 
-    piece = kv_hbm.shape[1] // PIECES
-
-    def value_copy(o, j):
-        at = pl.ds(j * piece, piece)
-        return pltpu.make_async_remote_copy(
-            kv_hbm.at[1, at, :, lanes_of(block_of[o])], (vn.at[core, at], vl.at[at], vo.at[at])[o - 1],
-            v_ssem.at[o - 1, j], v_rsem.at[o - 1, j], device_id={"tp": mate(t, o)}, device_id_type=MESH)
-
     key_moves = {o: key_copies(o) for o in (1, 2, 3)}
-    value_moves = [value_copy(o, j) for o in (3, 2) for j in range(PIECES)]
-    near_values = [value_copy(1, j) for j in range(PIECES)]
     for o in (2, 3, 1):
-        key_moves[o][1].start()
-    for o in (2, 3, 1):
-        key_moves[o][0].start()
-    for move in near_values:
-        move.start()
+        key_moves[o][PIECES].start()
+    for j in range(PIECES - 1):
+        for o in (2, 3, 1):
+            key_moves[o][j].start()
+    key_moves[1][PIECES - 1].start()
     own_cache = [
         pltpu.make_async_copy(kv_hbm.at[0, :, :, lanes_of(i)], kn.at[core], loc_sem.at[7]),
         pltpu.make_async_copy(sc_hbm.at[:, :, lanes_of(i)], scx.at[i], loc_sem.at[8]),
-        pltpu.make_async_copy(kv_hbm.at[1, :, :, lanes_of(i)], vn.at[core], loc_sem.at[9]),
     ]
+    for b in range(4):
+        at = pl.ds(128 * b, 128)
+        own_cache.append(pltpu.make_async_copy(kv_hbm.at[1, :, :, at], vown.at[b], loc_sem.at[11 + b]))
+        own_cache.append(pltpu.make_async_copy(sc_hbm.at[1, :, at], sv.at[b], loc_sem.at[15 + b]))
     for copy in own_cache:
         copy.start()
     loads[3].start()
@@ -265,12 +262,18 @@
     for o in (2, 1):
         q_share(o, 0).start()
     lax.fori_loop(1, ng, q_forward, 0)
-    for move in value_moves[:EARLY]:
-        move.start()
+    for o in (2, 3):
+        key_moves[o][PIECES - 1].start()
 
     fold_row = iota(fold.shape, 0)
     fold_lane = iota(fold.shape, 1)
     fold[...] = ones((fold_row // 128 == fold_lane // 32) & (fold_row % 32 == fold_lane % 32))
+    wide = 32 * ng
+    row_w = iota((128, wide), 0)
+    lane_w = iota((128, wide), 1)
+    hit = ((lane_w // 32).astype(F32) == src_col[:, 0:1]) & (lane_w % 4 == row_w // 32)
+    for b in range(8):
+        picks[b] = ones(hit & ((lane_w // 4) % 8 == b))
     diagonal = ones(row // 32 == lane // 32)
     stat[...] = jnp.zeros_like(stat)
     to_scalars.wait()
@@ -294,10 +297,10 @@
 
     own_cache[0].wait()
     own_cache[1].wait()
-    for kind in (0, 1):
-        key_moves[1][kind].wait_recv()
-    key_moves[2][1].wait_recv()
-    key_moves[3][1].wait_recv()
+    for move in key_moves[1]:
+        move.wait_recv()
+    key_moves[2][PIECES].wait_recv()
+    key_moves[3][PIECES].wait_recv()
     scf[...] = scx[...].astype(F32)
 
     def each(first, last, width, body):
@@ -326,8 +329,6 @@
         return 0
 
     lax.fori_loop(0, ng, hand_all, 0)
-    key_moves[2][0].wait_recv()
-    key_moves[3][0].wait_recv()
     pnew[...] = jnp.full(pnew.shape, -jnp.inf, F32)
 
     def far_arrival(k, _):
@@ -338,20 +339,19 @@
     first_new = (g - i + 4 * ng) % 4
     share = max(ng // 4, 1)
 
-    def score_new(j, _):
+    column = iota((128, 16), 1)
+    seen = (column <= iota((128, 16), 0) % 4) & (column < 4)
+    news = []
+    for j in range(share):
         k = lax.rem(first_new + 4 * j, ng)
         there, _ = slots(k)
         new = jnp.zeros((128, 16), F32)
         for n in range(4):
             new = new + nt(queries(n, there), qx[n, there, 32:48, :])
-        column = iota((128, 16), 1)
-        seen = (column <= iota((128, 16), 0) % 4) & (column < 4)
-        if ng < 4:
-            seen = seen & (there == i)
-        pnew[k] = jnp.where(seen, new, -jnp.inf)
-        return 0
-
-    lax.fori_loop(0, share, score_new, 0)
+        mine_too = seen & (there == i) if ng < 4 else seen
+        news.append((k, jnp.where(mine_too, new, -jnp.inf)))
+    for k, new in news:
+        pnew[k] = new
 
     def score_far(ks):
         done = []
@@ -366,12 +366,55 @@
             done.append((part, new, top, mass))
         both = stat[...]
         for k, (part, new, top, mass) in zip(ks, done):
-            prob[k] = part
+            px[i, k] = part.astype(BF16)
             pnew[k] = new
             both = jnp.where(lane == k, top, jnp.where(lane == ng + k, mass, both))
         stat[...] = both
 
-    each(0, ng, 2, score_far)
+    for o in (2, 3):
+        for move in key_moves[o][:PIECES]:
+            move.wait_recv()
+
+    def p_at(q):
+        return pl.ds(q * per, per)
+
+    def p_copy(o, q):
+        return pltpu.make_async_remote_copy(
+            px.at[i, p_at(q)], px.at[i, p_at(q)], p_ssem.at[o - 1, q], p_rsem.at[o - 1, q],
+            device_id={"tp": mate(t, o)}, device_id_type=MESH)
+
+    def p_arrival(o, q):
+        return pltpu.make_async_remote_copy(
+            px.at[i, p_at(q)], px.at[block_of[o], p_at(q)], p_ssem.at[o - 1, q], p_rsem.at[o - 1, q],
+            device_id={"tp": mate(t, o)}, device_id_type=MESH)
+
+    def p_relay(q):
+        return pltpu.make_async_remote_copy(
+            px.at[block_of[2], p_at(q)], px.at[block_of[2], p_at(q)], p_ssem.at[2, q], p_rsem.at[2, q],
+            device_id={"tp": mate(t, 1)}, device_id_type=MESH)
+
+    for q in range(chunks):
+        each(q * per, (q + 1) * per, 2, score_far)
+        if q < chunks - 1:
+            p_copy(2, q).start()
+            p_copy(1, q).start()
+    packed = jnp.zeros((128, 128), F32)
+    for j in range(share):
+        new = pnew[lax.rem(first_new + 4 * j, ng)]
+        packed = jnp.where(lane // 16 == j, jnp.concatenate([new] * 8, axis=1), packed)
+    pnp[i] = packed.astype(BF16)
+    pn_moves = [
+        pltpu.make_async_remote_copy(
+            pnp.at[i], pnp.at[i], pn_ssem.at[o - 1], pn_rsem.at[o - 1],
+            device_id={"tp": mate(t, o)}, device_id_type=MESH)
+        for o in (1, 2, 3)
+    ]
+    pn_arrivals = [
+        pltpu.make_async_remote_copy(
+            pnp.at[i], pnp.at[block_of[o]], pn_ssem.at[o - 1], pn_rsem.at[o - 1],
+            device_id={"tp": mate(t, o)}, device_id_type=MESH)
+        for o in (1, 2, 3)
+    ]
 
     st_send[...] = jnp.transpose(stat[...])[0 : 2 * ng, :]
     st_moves = [
@@ -382,16 +425,26 @@
     ]
     for o in (2, 1, 0):
         st_moves[o].start()
-    for move in value_moves[EARLY:]:
-        move.start()
+    for o in (2, 1, 0):
+        pn_moves[o].start()
+    p_copy(2, chunks - 1).start()
+    p_copy(1, chunks - 1).start()
+    for copy in own_cache[2:]:
+        copy.wait()
+    svf[...] = sv[...].astype(F32)
     for o in range(3):
         st_moves[o].wait_recv()
+        pn_arrivals[o].wait_recv()
     tops = [st_send[0:ng, :]] + [st_recv[o, 0:ng, :] for o in range(3)]
     masses = [st_send[ng : 2 * ng, :]] + [st_recv[o, ng : 2 * ng, :] for o in range(3)]
     top = jnp.maximum(jnp.maximum(tops[0], tops[1]), jnp.maximum(tops[2], tops[3]))
     mass = sum(masses[o] * jnp.exp(tops[o] - top) for o in range(4))
-    factor = jnp.exp(tops[0] - top) / mass
-    fac[...] = jnp.transpose(jnp.concatenate([factor, jnp.zeros((128 - ng, 128), F32)], axis=0))
+    for o in range(4):
+        facn[block_of[o]] = jnp.exp(tops[o] - top) / mass
+    factors = [facn[n] for n in range(4)]
+    if 4 * ng < 128:
+        factors.append(jnp.zeros((128 - 4 * ng, 128), F32))
+    fac[...] = jnp.transpose(jnp.concatenate(factors, axis=0))
 
     def keep(out):
         kept = jnp.zeros((32, 128), F32)
@@ -399,54 +452,27 @@
             kept = kept + jnp.where(lane[0:32] // 32 == c, out[32 * c : 32 * c + 32, :], 0.0)
         return kept
 
-    def value(ks, mates, first):
-        if first:
-            for k in ks:
-                column = jnp.sum(jnp.where(lane == k, fac[...], 0.0), axis=1, keepdims=True)
-                pb[k] = (prob[k] * column).astype(BF16)
+    def factor_of(n, k):
+        return jnp.sum(jnp.where(lane == n * ng + k, fac[...], 0.0), axis=1, keepdims=True)
+
+    def value(ks):
         kept = []
         for k in ks:
             there, ids = slots(k)
-            p = pb[k].astype(F32)
-            for o in mates:
-                weighted = (p * scale_rows(block_of[o], 1, ids)).astype(BF16)
-                held = [vn.at[core], vn.at[1 - core], vl, vo][o]
-                values = jnp.concatenate([held[ids[c]] for c in range(CAP)], axis=0)
-                kept.append((block_of[o], k, keep(nt(weighted, values))))
-        for n, k, out in kept:
-            acc[n, k] = acc[n, k] + out
-
-    def value_new(j, _):
-        k = lax.rem(first_new + 4 * j, ng)
-        there, _ = slots(k)
-        pn = pnew[k].astype(BF16)
-        for n in range(4):
-            both = qx[n, there, 32:48, :].astype(F32)
-            new_values = pltpu.roll(both, 12, 0).astype(BF16)
-            acc[n, k] = keep(nn(pn, new_values))
-        return 0
-
-    def scale_new(j, _):
-        k = lax.rem(first_new + 4 * j, ng)
-        column = jnp.sum(jnp.where(lane == k, fac[...], 0.0), axis=1, keepdims=True)
-        pnew[k] = pnew[k] * column
-        return 0
-
-    near_sum = pltpu.make_async_remote_copy(
-        acc.at[block_of[1]], ra.at[0], ha_ssem.at[0], ha_rsem.at[0],
-        device_id={"tp": mate(t, 1)}, device_id_type=MESH)
-
-    def far_sum(q):
-        at = pl.ds(q * per, per)
-        return pltpu.make_async_remote_copy(
-            acc.at[block_of[3], at], ra.at[1, at], ha_ssem.at[1 + q], ha_rsem.at[1 + q],
-            device_id={"tp": mate(t, 1)}, device_id_type=MESH)
-
-    def chip_sum(q):
-        at = pl.ds(q * per, per)
-        return pltpu.make_async_remote_copy(
-            sb.at[at], rb.at[at], hb_ssem.at[q], hb_rsem.at[q],
-            device_id={"tp": mate(t, 2)}, device_id_type=MESH)
+            out = jnp.zeros((128, 128), F32)
+            for n in range(4):
+                scales = jnp.concatenate(
+                    [jnp.broadcast_to(svf[n, pl.ds(ids[c], 1), :], (32, 128)) for c in range(CAP)], axis=0)
+                weighted = (px[n, k].astype(F32) * factor_of(n, k) * scales).astype(BF16)
+                values = jnp.concatenate([vown[n, ids[c]] for c in range(CAP)], axis=0)
+                out = out + nt(weighted, values)
+            n = there % 4
+            new_probs = (pnp[n].astype(F32) * factor_of(n, k)).astype(BF16)
+            both = pltpu.roll(qx[i, there, 32:48, :].astype(F32), 12, 0)
+            new_values = jnp.where(row // 16 == k // 4, jnp.concatenate([both] * 8, axis=0), 0.0).astype(BF16)
+            kept.append(keep(out + nn(new_probs, new_values)).astype(BF16))
+        for k, out in zip(ks, kept):
+            mix[k] = out
 
     def back_copy(k):
         there = lax.rem(g - k + ng, ng)
@@ -462,52 +488,26 @@
         back_copy(k).wait()
         return 0
 
-    def send_chip_sum(q):
-        at = pl.ds(q * per, per)
-        far_sum(q).wait()
-        sb[at] = (acc[block_of[2], at] + ra[1, at]).astype(BF16)
-        chip_sum(q).start()
-
-    def send_back(q):
-        at = pl.ds(q * per, per)
-        chip_sum(q).wait()
-        mix[at] = (acc[i, at] + ra[0, at] + rb[at].astype(F32)).astype(BF16)
+    def hand_on_p(q):
+        p_arrival(2, q).wait_recv()
+        p_relay(q).start()
+
+    hand_on_p(0)
+    for q in range(chunks):
+        if q + 1 < chunks:
+            hand_on_p(q + 1)
+        p_arrival(1, q).wait_recv()
+        p_arrival(3, q).wait_recv()
+        each(q * per, (q + 1) * per, 2, value)
         lax.fori_loop(max(q * per, 1), (q + 1) * per, back_start, 0)
-
-    acc[...] = jnp.zeros_like(acc)
-    lax.fori_loop(0, share, scale_new, 0)
-    lax.fori_loop(0, share, value_new, 0)
-    own_cache[2].wait()
-    for move in near_values:
-        move.wait_recv()
-    each(0, ng, 2, lambda ks: value(ks, (0, 1), True))
-    near_sum.start()
-    for move in value_moves[:PIECES]:
-        move.wait_recv()
-    for q in range(chunks):
-        each(q * per, (q + 1) * per, 4, lambda ks: value(ks, (3,), False))
-        far_sum(q).start()
-    for move in value_moves[PIECES:]:
-        move.wait_recv()
-    for q in range(chunks):
-        each(q * per, (q + 1) * per, 4, lambda ks: value(ks, (2,), False))
-        send_chip_sum(q)
-    near_sum.wait()
-    for q in range(chunks):
-        send_back(q)
     back[g] = mix[0]
     lax.fori_loop(1, ng, back_wait, 0)
 
-    wide = 32 * ng
-    row_w = iota((128, wide), 0)
-    lane_w = iota((128, wide), 1)
-    hit = ((lane_w // 32).astype(F32) == src_col[:, 0:1]) & (lane_w % 4 == row_w // 32)
     chosen = rank_col[...] == (lane // 32).astype(F32)
     slots_all = back[...].reshape(wide, 128)
     mixed = jnp.zeros((128, 256), F32)
     for b in range(8):
-        pick = ones(hit & ((lane_w // 4) % 8 == b))
-        rows_b = jnp.where(chosen, nn(pick, slots_all), 0.0).astype(BF16)
+        rows_b = jnp.where(chosen, nn(picks[b], slots_all), 0.0).astype(BF16)
         mixed = mixed + nn(rows_b, fold[128 * b : 128 * b + 128, :])
     mixed = mixed.astype(BF16)
 
@@ -612,10 +612,14 @@
     lax.fori_loop(1, ng, q_sent, 0)
     lax.fori_loop(0, ng, q_shared, 0)
     for o in (1, 2, 3):
-        key_moves[o][0].wait_send()
-        key_moves[o][1].wait_send()
+        for move in key_moves[o]:
+            move.wait_send()
         st_moves[o - 1].wait_send()
-    for move in near_values + value_moves:
+    for q in range(chunks):
+        p_copy(1, q).wait_send()
+        p_copy(2, q).wait_send()
+        p_relay(q).wait_send()
+    for move in pn_moves:
         move.wait_send()
 
 
@@ -661,24 +665,23 @@
         pltpu.VMEM((4, ng, 48, 128), BF16),
         pltpu.VMEM((2, particles, 32, 128), BF16),
         pltpu.VMEM((2, particles, 32, 128), BF16),
-        pltpu.VMEM((2, particles, 32, 128), BF16),
-        pltpu.VMEM((particles, 32, 128), BF16),
-        pltpu.VMEM((particles, 32, 128), BF16),
+        pltpu.VMEM((4, particles, 32, 128), BF16),
+        pltpu.VMEM((4, particles, 128), BF16),
+        pltpu.VMEM((4, particles, 128), F32),
         pltpu.VMEM((4, 2, particles, 128), BF16),
         pltpu.VMEM((4, 2, particles, 128), F32),
         pltpu.VMEM((ng, 128, 128), F32),
-        pltpu.VMEM((ng, 128, 128), BF16),
+        pltpu.VMEM((4, ng, 128, 128), BF16),
+        pltpu.VMEM((4, 128, 128), BF16),
         pltpu.VMEM((ng, 128, 16), F32),
         pltpu.VMEM((128, 128), F32),
         pltpu.VMEM((2 * ng, 128), F32),
         pltpu.VMEM((3, 2 * ng, 128), F32),
+        pltpu.VMEM((4, ng, 128), F32),
         pltpu.VMEM((128, 128), F32),
-        pltpu.VMEM((4, ng, 32, 128), F32),
-        pltpu.VMEM((2, ng, 32, 128), F32),
         pltpu.VMEM((ng, 32, 128), BF16),
         pltpu.VMEM((ng, 32, 128), BF16),
-        pltpu.VMEM((ng, 32, 128), BF16),
-        pltpu.VMEM((ng, 32, 128), BF16),
+        pltpu.VMEM((8, 128, 32 * ng), BF16),
         pltpu.VMEM((1024, 256), BF16),
         pltpu.VMEM((2, 8, rows, half), BF16),
         pltpu.VMEM((2, 8, rows, half), BF16),
@@ -688,14 +691,13 @@
         pltpu.VMEM((4, 2, rows, half // 2), F32),
         pltpu.VMEM((4, rows, half // 2), BF16),
         pltpu.VMEM((4, rows, half // 2), BF16),
-        dma((11,)),
-        dma((3, 2)), dma((3, 2)),
-        dma((3, PIECES)), dma((3, PIECES)),
+        dma((19,)),
+        dma((3, PIECES + 1)), dma((3, PIECES + 1)),
+        dma((3, MAX_CHUNKS)), dma((3, MAX_CHUNKS)),
+        dma((3,)), dma((3,)),
         dma((ng,)), dma((ng,)),
         dma((3, ng)), dma((3, ng)),
         dma((3,)), dma((3,)),
-        dma((1 + MAX_CHUNKS,)), dma((1 + MAX_CHUNKS,)),
-        dma((MAX_CHUNKS,)), dma((MAX_CHUNKS,)),
         dma((ng,)), dma((ng,)),
         dma((2, 8)), dma((2, 8)),
         dma((4, 6)), dma((4, 6)),
@@ -703,7 +705,7 @@
     ]
     out = pl.pallas_call(
         functools.partial(kernel, ng),
-        out_shape=jax.ShapeDtypeStruct((rows, cb), BF16),
+        out_shape=pltpu.VMEM((rows, cb), BF16),
         in_specs=[hbm] * 9,
         out_specs=vmem,
         scratch_shapes=scratch,

time: 75.5 us -> 73.9 us (0.979)
  local copies, waits for them, and re-layouts: 1.57 us -> 0.66 us
    unnamed x1, local copies, waits for them, and re-layouts: 1.57 us -> 0.66 us
where the time goes in v6:
time: 73.9 us; the launch traced here: 73.8 us
  Pallas kernels  73.1 us (99%)
    pallas_call x1, Pallas kernels, shards(): pl.pallas_call(functools.partial(kernel, ng), out_shape=pltpu.VMEM((rows,...  73.1 us

profile of v6, /device:TPU:2, one launch (start us, length us, event | category | flops | bytes accessed | tf_op | source)
XLA Modules:
  0.0 73.8 jit_solution(336706921509565000)
XLA Ops:
  0.0 73.1 %shard_map.91 = bf16[128,512]{1,0:T(8,128)(2,1)S(1)} custom-call(bf16[128,8192]{1,0:T(8,128)(2,1)} %bitcast.15, bf16[64,128]{1,0:T(8,128)(2,1)} %bitcast.18, bf16[256,8192]{1,0:T(8,128)(2,1)} %bitcast.13, bf16[64,8192]{1,0:T(8,128)(2,1)} %bitcast.16, bf16[256,8192]{1,0:T(8,128)(2,1)} %bitcast.14, bf16[2,32,32,512]{3,2,1,0:T(8,128)(2,1)} %kv_hbm.1, ...), custom_call_target="tpu_custom_call" | custom-call | tf_op jit(solution)/shard_map/pallas_call | solution.py:706
  73.1 0.7 copy.11

commit v7 on v6

--- a/solution.py
+++ b/solution.py
@@ -322,7 +322,7 @@
         for k, total in zip(ks, totals):
             prob[k] = total
 
-    each(0, ng, 2, score_near)
+    each(0, ng, 4, score_near)
 
     def hand_all(k, _):
         hand_on(k)
@@ -394,8 +394,8 @@
             device_id={"tp": mate(t, 1)}, device_id_type=MESH)
 
     for q in range(chunks):
-        each(q * per, (q + 1) * per, 2, score_far)
-        if q < chunks - 1:
+        each(q * per, (q + 1) * per, 4, score_far)
+        if q == 0:
             p_copy(2, q).start()
             p_copy(1, q).start()
     packed = jnp.zeros((128, 128), F32)
@@ -427,8 +427,9 @@
         st_moves[o].start()
     for o in (2, 1, 0):
         pn_moves[o].start()
-    p_copy(2, chunks - 1).start()
-    p_copy(1, chunks - 1).start()
+    for q in range(1, chunks):
+        p_copy(2, q).start()
+        p_copy(1, q).start()
     for copy in own_cache[2:]:
         copy.wait()
     svf[...] = sv[...].astype(F32)
@@ -498,7 +499,7 @@
             hand_on_p(q + 1)
         p_arrival(1, q).wait_recv()
         p_arrival(3, q).wait_recv()
-        each(q * per, (q + 1) * per, 2, value)
+        each(q * per, (q + 1) * per, 4, value)
         lax.fori_loop(max(q * per, 1), (q + 1) * per, back_start, 0)
     back[g] = mix[0]
     lax.fori_loop(1, ng, back_wait, 0)

time: 73.9 us -> 73.6 us (level)
  no operation moved by 1% of the time
where the time goes in v7:
time: 73.6 us
  Pallas kernels  72.9 us (99%)
    pallas_call x1, Pallas kernels, shards(): pl.pallas_call(functools.partial(kernel, ng), out_shape=pltpu.VMEM((rows,...  72.9 us

profile of v7, /device:TPU:2, one launch (start us, length us, event | category | flops | bytes accessed | tf_op | source)
XLA Modules:
  0.0 73.6 jit_solution(6848851328325984273)
XLA Ops:
  0.0 72.9 %shard_map.91 = bf16[128,512]{1,0:T(8,128)(2,1)S(1)} custom-call(bf16[128,8192]{1,0:T(8,128)(2,1)} %bitcast.15, bf16[64,128]{1,0:T(8,128)(2,1)} %bitcast.18, bf16[256,8192]{1,0:T(8,128)(2,1)} %bitcast.13, bf16[64,8192]{1,0:T(8,128)(2,1)} %bitcast.16, bf16[256,8192]{1,0:T(8,128)(2,1)} %bitcast.14, bf16[2,32,32,512]{3,2,1,0:T(8,128)(2,1)} %kv_hbm.1, ...), custom_call_target="tpu_custom_call" | custom-call | tf_op jit(solution)/shard_map/pallas_call | solution.py:707
  72.9 0.7 copy.11
